TPU v7x, 128 devices: a whole 4x4x4 slice. The times are simulated.
128 devices in a mesh: gx: 16 (over x_lo, z, core), gy: 8 (over x_hi, y).
Axes of the slice: x: 4 (x_hi: 2, x_lo: 2; x = x_hi * 2 + x_lo), y: 4, z: 4, core: 2. Of those that a mesh axis runs over, the one named last changes fastest.
Arguments:
- basin_velocity: float32 [3, 16, 1024, 1024], P(None, None, 'gx', 'gy'), may hold values from -6 to 6
- basin_stress: float32 [6, 16, 1024, 1024], P(None, None, 'gx', 'gy'), may hold values from -6 to 6
- basin_media: float32 [3, 16, 1024, 1024], P(None, None, 'gx', 'gy'), may hold values from 0.5 to 2
- box_velocity: float32 [3, 8, 1024, 1024], P(None, None, 'gx', 'gy'), may hold values from -6 to 6
- box_stress: float32 [6, 8, 1024, 1024], P(None, None, 'gx', 'gy'), may hold values from -6 to 6
- zone_ids: int32 [8, 1024, 1024], P(None, 'gx', 'gy'), may hold values from 0 to 7
- zone_media: float32 [3, 8], replicated, may hold values from 0.5 to 2
- corridor_tile: int32 [16, 8, 8192, 1], P('gx'), may hold values from 0 to 7; in each aligned block of 8192 rows (0 to 8191, 8192 to 16383, ..., all dimensions but the last counted through in order) at most 2048 rows name the same one
- corridor_cell: int32 [16, 8, 8192], P('gx'), may hold values from 0 to 8191
- drm_stiff: float32 [16, 8, 64, 128, 128], P('gx', 'gy'), may hold values from -0.5 to 0.5
- drm_mass: float32 [16, 8, 64, 128, 128], P('gx', 'gy'), may hold values from -0.5 to 0.5
Outputs:
- basin_velocity_next: float32 [3, 16, 1024, 1024], P(None, None, 'gx', 'gy')
- basin_stress_next: float32 [6, 16, 1024, 1024], P(None, None, 'gx', 'gy')
- box_velocity_next: float32 [3, 8, 1024, 1024], P(None, None, 'gx', 'gy')
- box_stress_next: float32 [6, 8, 1024, 1024], P(None, None, 'gx', 'gy')
Inputs may be any that keep to these rules, and one draw needn't show every extreme that they name: `corridor_tile`: within the 8192 rows of one owner (one index pair of the first two dimensions) no tile is named by more than 2048 rows, and in every draw some owner has a tile named by exactly 2048 rows.
All inputs are finite; a program needn't handle non-finite values.
Results may differ from a plain program's by a relative error of at most 0.0001.
Values sent between devices are 32-bit elements; how exact they have to be, the bound alone decides.
No kernel may reach another device: no remote copies, remote signals or barrier semaphores. Data moves between devices by JAX's collectives and lax.ppermute only.
A program may use at most 128 MiB of HBM per device.

v0:
```python
import math

import jax
import jax.numpy as jnp
from jax import lax
from jax.sharding import PartitionSpec as P

NZ = 16
STEPS = 2
ZR = 8
ZONES = 8
CAP = 2048


COURANT = 0.12
FOURTH_NEAR = 9.0 / 8.0
FOURTH_FAR = 1.0 / 24.0


def extended(value, sides, width):
    for axis, dim in sides:
        peers, length = (lax.axis_size(axis), value.shape[dim])
        up = [(i, (i + 1) % peers) for i in range(peers - 1)]
        down = [(j, i) for i, j in up]
        last = lax.slice_in_dim(value, length - width, length, axis=dim)
        first = lax.slice_in_dim(value, 0, width, axis=dim)
        before = lax.ppermute(last, axis, up)
        after = lax.ppermute(first, axis, down)
        value = jnp.concatenate([before, value, after], axis=dim)
    return value


def forward_diff(padded, dimension):
    length = padded.shape[dimension] - 4

    def window(offset):
        return lax.slice_in_dim(padded, offset, offset + length, axis=dimension)

    return FOURTH_NEAR * (window(3) - window(2)) - FOURTH_FAR * (window(4) - window(1))


def backward_diff(padded, dimension):
    length = padded.shape[dimension] - 4

    def window(offset):
        return lax.slice_in_dim(padded, offset, offset + length, axis=dimension)

    return FOURTH_NEAR * (window(2) - window(1)) - FOURTH_FAR * (window(3) - window(0))


def new_velocity(velocity, buoyancy, slopes):
    comp_x = velocity[0] + COURANT * buoyancy * (slopes[0] + slopes[1] + slopes[2])
    comp_y = velocity[1] + COURANT * buoyancy * (slopes[3] + slopes[4] + slopes[5])
    comp_z = velocity[2] + COURANT * buoyancy * (slopes[6] + slopes[7] + slopes[8])
    return jnp.stack([comp_x, comp_y, comp_z])


def new_stress(stress, material, slopes):
    lame_first = material[0]
    shear_mod = material[1]
    modulus = lame_first + 2.0 * shear_mod
    along_x, along_y, along_z = (slopes[0], slopes[1], slopes[2])
    comp_xx = stress[0] + COURANT * (modulus * along_x + lame_first * (along_y + along_z))
    comp_xz = stress[1] + COURANT * shear_mod * (slopes[5] + slopes[6])
    comp_xy = stress[2] + COURANT * shear_mod * (slopes[3] + slopes[4])
    comp_yz = stress[3] + COURANT * shear_mod * (slopes[7] + slopes[8])
    comp_yy = stress[4] + COURANT * (modulus * along_y + lame_first * (along_x + along_z))
    comp_zz = stress[5] + COURANT * (modulus * along_z + lame_first * (along_x + along_y))
    return jnp.stack([comp_xx, comp_xz, comp_xy, comp_yz, comp_yy, comp_zz])


def depth_derivative(values, forward):
    upper_part = jnp.pad(values[:NZ], ((2, 2), (0, 0), (0, 0)))
    lower_part = jnp.pad(values[NZ:], ((2, 2), (0, 0), (0, 0)))
    difference = forward_diff if forward else backward_diff
    return jnp.concatenate([difference(upper_part, 0), difference(lower_part, 0)], axis=0)


def select_cells(values, group_index, lane_index):
    components, group_count, lane_count = values.shape
    total = lane_index.shape[0]
    width_block = math.gcd(1024, total)
    flattened = values.reshape(components * group_count, lane_count)

    def one_block(pair):
        lane_part, group_part = pair
        lane_onehot = (
            lax.broadcasted_iota(jnp.int32, (lane_count, width_block), 0) == lane_part[None, :]
        ).astype(jnp.float32)
        spread = jnp.dot(flattened, lane_onehot, precision=lax.Precision.HIGHEST)
        spread = spread.reshape(components, group_count, width_block)
        group_onehot = (
            lax.broadcasted_iota(jnp.int32, (group_count, width_block), 0) == group_part[None, :]
        ).astype(jnp.float32)
        return jnp.sum(spread * group_onehot[None], axis=1)

    pieces = lax.map(
        one_block, (lane_index.reshape(-1, width_block), group_index.reshape(-1, width_block))
    )
    return pieces.transpose(1, 0, 2).reshape(components, total)


def shards(
    basin_velocity,
    basin_stress,
    basin_media,
    box_velocity,
    box_stress,
    zone_ids,
    zone_media,
    corridor_tile,
    corridor_cell,
    drm_stiff,
    drm_mass,
):
    box_media = jnp.broadcast_to(zone_media[:, 0][:, None, None, None], (3,) + zone_ids.shape)
    for number in range(1, ZONES):
        box_media = jnp.where(
            (zone_ids == number)[None], zone_media[:, number][:, None, None, None], box_media
        )
    velocity = jnp.concatenate([basin_velocity, box_velocity], axis=1)
    stress = jnp.concatenate([basin_stress, box_stress], axis=1)
    material = jnp.concatenate([basin_media, box_media], axis=1)
    buoyancy = material[2]
    tile_cols = basin_velocity.shape[3]
    column = lax.axis_index("gy")
    owners = lax.axis_size("gy")
    tiles_all = corridor_tile[0, :, :, 0]
    cells_all = corridor_cell[0]
    own_tiles = lax.dynamic_index_in_dim(tiles_all, column, 0, keepdims=False)
    chosen = tiles_all == column
    inclusive = jnp.cumsum(chosen.astype(jnp.int32), axis=1)
    slot_keys = jnp.where(chosen, inclusive - 1, -1)
    filled_count = inclusive[:, -1]
    slot_block = math.gcd(256, CAP)
    first_slots = jnp.arange(0, CAP, slot_block, dtype=jnp.int32)

    def owner_slots(pair):
        owner_keys, owner_cells = pair

        def slot_cells(first_slot):
            slot_ids = first_slot + lax.broadcasted_iota(jnp.int32, (slot_block, 1), 0)
            matched = owner_keys[None, :] == slot_ids
            return jnp.sum(jnp.where(matched, owner_cells[None, :], 0), axis=1)

        return lax.map(slot_cells, first_slots).reshape(CAP)

    slot_cell = lax.map(owner_slots, (slot_keys, cells_all))
    slot_ids_all = lax.broadcasted_iota(jnp.int32, (owners, CAP), 1)
    filled = (slot_ids_all < filled_count[:, None]).astype(jnp.float32).reshape(-1)
    slot_cell = slot_cell.reshape(-1)
    slot_rows = slot_cell // tile_cols
    slot_lanes = slot_cell % tile_cols
    tile_ids = lax.broadcasted_iota(jnp.int32, (owners, own_tiles.shape[0]), 0)
    matches = (own_tiles[None, :] == tile_ids).astype(jnp.int32)
    own_ranks = jnp.sum(matches * (jnp.cumsum(matches, axis=1) - 1), axis=0)

    def deliver(layer_values):
        packed = select_cells(layer_values, slot_rows, slot_lanes) * filled[None, :]
        received = lax.all_to_all(
            packed.reshape(3, owners, CAP), "gy", split_axis=1, concat_axis=1, tiled=True
        )
        return select_cells(received, own_tiles, own_ranks)

    stiffness = drm_stiff[0, 0]
    inertia = drm_mass[0, 0]
    groups = stiffness.shape[0]
    group_rows = stiffness.shape[1]
    bottom = velocity.shape[1] - 1
    previous = deliver(basin_velocity[:, ZR])
    for number in range(STEPS):
        rims_x = extended(stress[0:3], (("gx", 2),), 2)
        rims_y = extended(stress[2:5], (("gy", 3),), 2)
        slopes = (
            forward_diff(rims_x[0], 1),
            backward_diff(rims_y[0], 2),
            depth_derivative(stress[1], False),
            backward_diff(rims_x[2], 1),
            forward_diff(rims_y[2], 2),
            depth_derivative(stress[3], False),
            backward_diff(rims_x[1], 1),
            backward_diff(rims_y[1], 2),
            depth_derivative(stress[5], True),
        )
        velocity = new_velocity(velocity, buoyancy, slopes)
        current = deliver(velocity[:, ZR])
        present = current.reshape(3, groups, group_rows)
        change = ((current - previous) / COURANT).reshape(3, groups, group_rows)
        stiff_part = jnp.einsum("gab,cgb->cga", stiffness, present, precision=lax.Precision.HIGHEST)
        mass_part = jnp.einsum("gab,cgb->cga", inertia, change, precision=lax.Precision.HIGHEST)
        summed = -(stiff_part + mass_part)
        velocity = velocity.at[:, bottom].add(COURANT * buoyancy[bottom] * summed)
        previous = current
        along_x = extended(velocity, (("gx", 2),), 2)
        along_y = extended(velocity, (("gy", 3),), 2)
        slopes = (
            backward_diff(along_x[0], 1),
            backward_diff(along_y[1], 2),
            depth_derivative(velocity[2], False),
            forward_diff(along_y[0], 2),
            forward_diff(along_x[1], 1),
            depth_derivative(velocity[0], True),
            forward_diff(along_x[2], 1),
            depth_derivative(velocity[1], True),
            forward_diff(along_y[2], 2),
        )
        stress = new_stress(stress, material, slopes)
    return (velocity[:, :NZ], stress[:, :NZ], velocity[:, NZ:], stress[:, NZ:])


def solution(mesh):
    return jax.shard_map(
        shards,
        mesh=mesh,
        in_specs=(
            P(None, None, "gx", "gy"),
            P(None, None, "gx", "gy"),
            P(None, None, "gx", "gy"),
            P(None, None, "gx", "gy"),
            P(None, None, "gx", "gy"),
            P(None, "gx", "gy"),
            P(),
            P("gx", None, None, None),
            P("gx", None, None),
            P("gx", "gy", None, None, None),
            P("gx", "gy", None, None, None),
        ),
        out_specs=(
            P(None, None, "gx", "gy"),
            P(None, None, "gx", "gy"),
            P(None, None, "gx", "gy"),
            P(None, None, "gx", "gy"),
        ),
        check_vma=False,
    )
```

profile of v0, /device:TPU:26, one launch (start us, length us, event | category | flops | bytes accessed | tf_op | source)
XLA Modules:
  0.0 678.1 jit_solution(680991380509668390)
XLA Ops:
  5.9 5.8 collective-permute-start.1
  21.2 6.9 %collective-permute-start.2 = (f32[3,24,64,2]{2,1,3,0:T(8,128)}, f32[3,24,64,2]{2,1,3,0:T(8,128)}, u32[]{:S(2)}, u32[]{:S(2)}) collective-permute-start(f32[3,24,64,2]{2,1,3,0:T(8,128)} %copy.152), channel_id=1, source_target_pairs={{0,1},{1,2},{2,3},{3,4},{4,5},{5,6},{6,7},{8,9},{9,10},{10,11},{11... | collective-permute-start | bytes 110600 | tf_op jit(solution)/shard_map/ppermute | solution.py:27
  45.6 166.5 %while.91 = (s32[]{:T(128)}, s32[8,2048]{1,0:T(8,128)}, s32[8,8192]{1,0:T(8,128)S(1)}, s32[8,8192]{1,0:T(8,128)}, s32[]{:T(128)}, /*index=5*/s32[]{:T(128)}, s32[]{:T(128)}, s32[]{:T(128)}) while((s32[]{:T(128)}, s32[8,2048]{1,0:T(8,128)}, s32[8,8192]{1,0:T(8,128)S(1)}, s32[8,8192]{1,0:T(8,128)}, s32[]{:T(128)}, ...), condition=%wide.region_9.10_spmd.clone, body=%wide.region_5.9_spmd.clone.sunk | while | flops 6291468 | bytes 234798 | solution.py:148
  46.6 18.3 %while.92 = (s32[]{:T(128)}, s32[8,256]{1,0:T(8,128)S(1)}, s32[8192]{0:T(1024)S(1)}, s32[8]{0:T(128)S(1)}, s32[8192]{0:T(1024)S(1)}, /*index=5*/s32[]{:T(128)}, s32[]{:T(128)}) while((s32[]{:T(128)}, s32[8,256]{1,0:T(8,128)S(1)}, s32[8192]{0:T(1024)S(1)}, s32[8]{0:T(128)S(1)}, s32[8192]{0:T(1024)S(1)}, /*index=5*/s32[]{:T(128)}, ...), condition=%wide.region_8.8_spmd, body=%wide.region_6.7_spmd.sunk | while | flops 6291458 | bytes 70761 | solution.py:146
  67.4 18.3 %while.92 = (s32[]{:T(128)}, s32[8,256]{1,0:T(8,128)S(1)}, s32[8192]{0:T(1024)S(1)}, s32[8]{0:T(128)S(1)}, s32[8192]{0:T(1024)S(1)}, /*index=5*/s32[]{:T(128)}, s32[]{:T(128)}) while((s32[]{:T(128)}, s32[8,256]{1,0:T(8,128)S(1)}, s32[8192]{0:T(1024)S(1)}, s32[8]{0:T(128)S(1)}, s32[8192]{0:T(1024)S(1)}, /*index=5*/s32[]{:T(128)}, ...), condition=%wide.region_8.8_spmd, body=%wide.region_6.7_spmd.sunk | while | flops 6291458 | bytes 70761 | solution.py:146
  88.2 18.3 %while.92 = (s32[]{:T(128)}, s32[8,256]{1,0:T(8,128)S(1)}, s32[8192]{0:T(1024)S(1)}, s32[8]{0:T(128)S(1)}, s32[8192]{0:T(1024)S(1)}, /*index=5*/s32[]{:T(128)}, s32[]{:T(128)}) while((s32[]{:T(128)}, s32[8,256]{1,0:T(8,128)S(1)}, s32[8192]{0:T(1024)S(1)}, s32[8]{0:T(128)S(1)}, s32[8192]{0:T(1024)S(1)}, /*index=5*/s32[]{:T(128)}, ...), condition=%wide.region_8.8_spmd, body=%wide.region_6.7_spmd.sunk | while | flops 6291458 | bytes 70761 | solution.py:146
  109.1 18.3 %while.92 = (s32[]{:T(128)}, s32[8,256]{1,0:T(8,128)S(1)}, s32[8192]{0:T(1024)S(1)}, s32[8]{0:T(128)S(1)}, s32[8192]{0:T(1024)S(1)}, /*index=5*/s32[]{:T(128)}, s32[]{:T(128)}) while((s32[]{:T(128)}, s32[8,256]{1,0:T(8,128)S(1)}, s32[8192]{0:T(1024)S(1)}, s32[8]{0:T(128)S(1)}, s32[8192]{0:T(1024)S(1)}, /*index=5*/s32[]{:T(128)}, ...), condition=%wide.region_8.8_spmd, body=%wide.region_6.7_spmd.sunk | while | flops 6291458 | bytes 70761 | solution.py:146
  129.9 18.3 %while.92 = (s32[]{:T(128)}, s32[8,256]{1,0:T(8,128)S(1)}, s32[8192]{0:T(1024)S(1)}, s32[8]{0:T(128)S(1)}, s32[8192]{0:T(1024)S(1)}, /*index=5*/s32[]{:T(128)}, s32[]{:T(128)}) while((s32[]{:T(128)}, s32[8,256]{1,0:T(8,128)S(1)}, s32[8192]{0:T(1024)S(1)}, s32[8]{0:T(128)S(1)}, s32[8192]{0:T(1024)S(1)}, /*index=5*/s32[]{:T(128)}, ...), condition=%wide.region_8.8_spmd, body=%wide.region_6.7_spmd.sunk | while | flops 6291458 | bytes 70761 | solution.py:146
  150.7 18.3 %while.92 = (s32[]{:T(128)}, s32[8,256]{1,0:T(8,128)S(1)}, s32[8192]{0:T(1024)S(1)}, s32[8]{0:T(128)S(1)}, s32[8192]{0:T(1024)S(1)}, /*index=5*/s32[]{:T(128)}, s32[]{:T(128)}) while((s32[]{:T(128)}, s32[8,256]{1,0:T(8,128)S(1)}, s32[8192]{0:T(1024)S(1)}, s32[8]{0:T(128)S(1)}, s32[8192]{0:T(1024)S(1)}, /*index=5*/s32[]{:T(128)}, ...), condition=%wide.region_8.8_spmd, body=%wide.region_6.7_spmd.sunk | while | flops 6291458 | bytes 70761 | solution.py:146
  171.5 18.3 %while.92 = (s32[]{:T(128)}, s32[8,256]{1,0:T(8,128)S(1)}, s32[8192]{0:T(1024)S(1)}, s32[8]{0:T(128)S(1)}, s32[8192]{0:T(1024)S(1)}, /*index=5*/s32[]{:T(128)}, s32[]{:T(128)}) while((s32[]{:T(128)}, s32[8,256]{1,0:T(8,128)S(1)}, s32[8192]{0:T(1024)S(1)}, s32[8]{0:T(128)S(1)}, s32[8192]{0:T(1024)S(1)}, /*index=5*/s32[]{:T(128)}, ...), condition=%wide.region_8.8_spmd, body=%wide.region_6.7_spmd.sunk | while | flops 6291458 | bytes 70761 | solution.py:146
  192.3 18.3 %while.92 = (s32[]{:T(128)}, s32[8,256]{1,0:T(8,128)S(1)}, s32[8192]{0:T(1024)S(1)}, s32[8]{0:T(128)S(1)}, s32[8192]{0:T(1024)S(1)}, /*index=5*/s32[]{:T(128)}, s32[]{:T(128)}) while((s32[]{:T(128)}, s32[8,256]{1,0:T(8,128)S(1)}, s32[8192]{0:T(1024)S(1)}, s32[8]{0:T(128)S(1)}, s32[8192]{0:T(1024)S(1)}, /*index=5*/s32[]{:T(128)}, ...), condition=%wide.region_8.8_spmd, body=%wide.region_6.7_spmd.sunk | while | flops 6291458 | bytes 70761 | solution.py:146
  214.5 20.0 %while.86 = (s32[]{:T(128)}, f32[16,3,1024]{2,1,0:T(4,128)}, s32[16,1024]{1,0:T(8,128)S(1)}, f32[192,128]{1,0:T(8,128)S(1)}, s32[16,1024]{1,0:T(8,128)S(1)}, /*index=5*/s32[]{:T(128)}) while((s32[]{:T(128)}, f32[16,3,1024]{2,1,0:T(4,128)}, s32[16,1024]{1,0:T(8,128)S(1)}, f32[192,128]{1,0:T(8,128)S(1)}, s32[16,1024]{1,0:T(8,128)S(1)}, ...), condition=%wide.region_18.19_spmd, body=%wide.region_16.18_spmd.sunk | while | flops 302642176 | bytes 2261077 | solution.py:97
  253.5 5.0 pad_maximum_fusion
  270.9 23.3 %while.84 = (s32[]{:T(128)}, f32[16,3,1024]{2,1,0:T(4,128)S(1)}, s32[16,1024]{1,0:T(8,128)}, f32[192,128]{1,0:T(8,128)S(1)}, s32[16,1024]{1,0:T(8,128)}, /*index=5*/s32[]{:T(128)}) while((s32[]{:T(128)}, f32[16,3,1024]{2,1,0:T(4,128)S(1)}, s32[16,1024]{1,0:T(8,128)}, f32[192,128]{1,0:T(8,128)S(1)}, s32[16,1024]{1,0:T(8,128)}, ...), condition=%wide.region_12.13_spmd, body=%wide.region_10.12_spmd.sunk | while | flops 302642176 | bytes 2265173 | solution.py:97
  298.4 4.5 all-to-all-start.1
  309.9 5.7 all-to-all-start
  317.4 35.8 %while.87 = (s32[]{:T(128)}, f32[8,3,1024]{2,1,0:T(4,128)S(1)}, s32[8,1024]{1,0:T(8,128)}, f32[24,2048]{1,0:T(8,128)}, s32[8,1024]{1,0:T(8,128)}, /*index=5*/s32[]{:T(128)}) while((s32[]{:T(128)}, f32[8,3,1024]{2,1,0:T(4,128)S(1)}, s32[8,1024]{1,0:T(8,128)}, f32[24,2048]{1,0:T(8,128)}, s32[8,1024]{1,0:T(8,128)}, ...), condition=%wide.region_21.22_spmd, body=%wide.region_19.21_spmd.sunk | while | flops 606139392 | bytes 331861 | solution.py:97
  322.7 3.6 fusion.374
  336.2 3.6 fusion.374
  349.6 3.6 fusion.374
  354.1 35.9 %while.85 = (s32[]{:T(128)}, f32[8,3,1024]{2,1,0:T(4,128)S(1)}, s32[8,1024]{1,0:T(8,128)}, f32[24,2048]{1,0:T(8,128)}, s32[8,1024]{1,0:T(8,128)}, /*index=5*/s32[]{:T(128)}) while((s32[]{:T(128)}, f32[8,3,1024]{2,1,0:T(4,128)S(1)}, s32[8,1024]{1,0:T(8,128)}, f32[24,2048]{1,0:T(8,128)}, s32[8,1024]{1,0:T(8,128)}, ...), condition=%wide.region_15.16_spmd, body=%wide.region_13.15_spmd.sunk | while | flops 606139392 | bytes 331861 | solution.py:97
  363.9 3.6 fusion.368
  372.9 3.6 fusion.368
  377.3 3.6 fusion.368
  386.3 3.6 fusion.368
  390.0 8.6 %fusion.31 = f32[64,3,128]{2,1,0:T(4,128)S(1)} fusion(f32[1,1,64,128,128]{4,3,2,1,0:T(8,128)} %param.41, f32[3,64,128]{2,0,1:T(4,128)S(1)} %bitcast.441, f32[3,64,128]{2,0,1:T(4,128)S(1)} %bitcast.450), kind=kOutput, calls=%fused_computation.72 | convolution fusion | flops 37797888 | bytes 4489216 | tf_op jit(solution)/shard_map/gab,cgb->cga/dot_general | solution.py:190
  398.6 6.7 fusion.52
  407.2 4.9 fusion.332
  416.3 3.7 copy.173
  420.0 3.7 copy.174
  426.4 6.7 collective-permute-start.6
  438.7 6.0 collective-permute-start.5
  450.8 4.3 pad_maximum_fusion.1
  470.5 5.8 collective-permute-start.9
  491.1 7.9 %collective-permute-start.10 = (f32[3,24,64,2]{2,1,3,0:T(8,128)}, f32[3,24,64,2]{2,1,3,0:T(8,128)}, u32[]{:S(2)}, u32[]{:S(2)}) collective-permute-start(f32[3,24,64,2]{2,1,3,0:T(8,128)} %copy.184), channel_id=1, source_target_pairs={{0,1},{1,2},{2,3},{3,4},{4,5},{5,6},{6,7},{8,9},{9,10},{10,11},{11... | collective-permute-start | bytes 110600 | tf_op jit(solution)/shard_map/ppermute | solution.py:27
  507.2 5.1 pad_maximum_fusion.2
  520.6 32.5 %while.88 = (s32[]{:T(128)}, f32[16,3,1024]{2,1,0:T(4,128)}, s32[16,1024]{1,0:T(8,128)}, f32[192,128]{1,0:T(8,128)S(1)}, s32[16,1024]{1,0:T(8,128)}, /*index=5*/s32[]{:T(128)}) while((s32[]{:T(128)}, f32[16,3,1024]{2,1,0:T(4,128)}, s32[16,1024]{1,0:T(8,128)}, f32[192,128]{1,0:T(8,128)S(1)}, s32[16,1024]{1,0:T(8,128)}, ...), condition=%wide.region_24.25_spmd, body=%wide.region_22.24_spmd.sunk | while | flops 302642176 | bytes 2261077 | solution.py:97
  556.0 13.7 %all_to_all.15 = f32[3,8,2048]{2,0,1:T(4,128)S(1)} all-to-all(f32[3,8,2048]{2,0,1:T(4,128)S(1)} %copy.190), channel_id=1, replica_groups=mesh['gx'=16,'gy'=8] {'gy'}, dimensions={1} | all-to-all | bytes 393216 | tf_op jit(solution)/shard_map/all_to_all | solution.py:160
  570.6 35.8 %while.89 = (s32[]{:T(128)}, f32[8,3,1024]{2,1,0:T(4,128)S(1)}, s32[8,1024]{1,0:T(8,128)}, f32[24,2048]{1,0:T(8,128)}, s32[8,1024]{1,0:T(8,128)}, /*index=5*/s32[]{:T(128)}) while((s32[]{:T(128)}, f32[8,3,1024]{2,1,0:T(4,128)S(1)}, s32[8,1024]{1,0:T(8,128)}, f32[24,2048]{1,0:T(8,128)}, s32[8,1024]{1,0:T(8,128)}, ...), condition=%wide.region_27.28_spmd, body=%wide.region_25.27_spmd.sunk | while | flops 606139392 | bytes 331861 | solution.py:97
  575.9 3.6 fusion.380
  580.4 3.6 fusion.380
  589.3 3.6 fusion.380
  593.8 3.6 fusion.380
  606.4 8.6 %fusion.29 = f32[64,3,128]{2,1,0:T(4,128)S(1)} fusion(f32[1,1,64,128,128]{4,3,2,1,0:T(8,128)} %param.41, f32[3,64,128]{2,0,1:T(4,128)S(1)} %bitcast.444, f32[3,64,128]{2,0,1:T(4,128)S(1)} %bitcast.443), kind=kOutput, calls=%fused_computation.70 | convolution fusion | flops 37797888 | bytes 4489216 | tf_op jit(solution)/shard_map/gab,cgb->cga/dot_general | solution.py:190
  615.1 6.6 fusion.33
  637.2 6.9 %collective-permute-start.14 = (f32[3,24,64,2]{2,1,3,0:T(8,128)}, f32[3,24,64,2]{2,1,3,0:T(8,128)}, u32[]{:S(2)}, u32[]{:S(2)}) collective-permute-start(f32[3,24,64,2]{2,1,3,0:T(8,128)} %copy.194), channel_id=1, source_target_pairs={{0,1},{1,2},{2,3},{3,4},{4,5},{5,6},{6,7},{8,9},{9,10},{10,11},{11... | collective-permute-start | bytes 110600 | tf_op jit(solution)/shard_map/ppermute | solution.py:27
  648.9 6.0 collective-permute-start.13
  660.2 4.3 pad_maximum_fusion.3
  (939 shorter events, 494.4 us)
Async XLA Ops:
  3.2 10.9 %copy-start = (f32[6,24,64,128]{3,2,1,0:T(8,128)}, f32[6,24,64,128]{3,2,1,0:T(8,128)S(1)}, u32[]{:S(2)}) copy-start(f32[6,24,64,128]{3,2,1,0:T(8,128)S(1)} %constant_dynamic-update-slice_fusion.2) | copy-start | bytes 14155780
  4.0 254.8 %collective-permute-start = (f32[3,24,2,128]{3,2,1,0:T(2,128)}, f32[3,24,2,128]{3,2,1,0:T(2,128)}, u32[]{:S(2)}, u32[]{:S(2)}) collective-permute-start(f32[3,24,2,128]{3,2,1,0:T(2,128)} %get-tuple-element.393), channel_id=1, source_target_pairs={{0,8},{8,16},{16,24},{24,32},{32,40},{40,48},{48,56},{56,64},{64,7... | collective-permute-start | bytes 221192 | tf_op jit(solution)/shard_map/ppermute | solution.py:27
  5.9 252.8 %collective-permute-start.1 = (f32[3,24,2,128]{3,2,1,0:T(2,128)}, f32[3,24,2,128]{3,2,1,0:T(2,128)}, u32[]{:S(2)}, u32[]{:S(2)}) collective-permute-start(f32[3,24,2,128]{3,2,1,0:T(2,128)} %get-tuple-element.394), channel_id=1, source_target_pairs={{8,0},{16,8},{24,16},{32,24},{40,32},{48,40},{56,48},{64,56},{72,6... | collective-permute-start | bytes 221192 | tf_op jit(solution)/shard_map/ppermute | solution.py:28
  17.1 233.3 %collective-permute-start.3 = (f32[3,24,64,2]{2,1,3,0:T(8,128)}, f32[3,24,64,2]{2,1,3,0:T(8,128)}, u32[]{:S(2)}, u32[]{:S(2)}) collective-permute-start(f32[3,24,64,2]{2,1,3,0:T(8,128)} %copy.153), channel_id=1, source_target_pairs={{1,0},{2,1},{3,2},{4,3},{5,4},{6,5},{7,6},{9,8},{10,9},{11,10},{12... | collective-permute-start | bytes 110600 | tf_op jit(solution)/shard_map/ppermute | solution.py:28
  21.2 11.7 %copy-start.30 = (f32[3,16,64,128]{3,2,1,0:T(8,128)S(1)}, f32[3,16,64,128]{3,2,1,0:T(8,128)}, u32[]{:S(2)}) copy-start(f32[3,16,64,128]{3,2,1,0:T(8,128)} %param.31) | copy-start | bytes 4718596
  21.2 226.2 %collective-permute-start.2 = (f32[3,24,64,2]{2,1,3,0:T(8,128)}, f32[3,24,64,2]{2,1,3,0:T(8,128)}, u32[]{:S(2)}, u32[]{:S(2)}) collective-permute-start(f32[3,24,64,2]{2,1,3,0:T(8,128)} %copy.152), channel_id=1, source_target_pairs={{0,1},{1,2},{2,3},{3,4},{4,5},{5,6},{6,7},{8,9},{9,10},{10,11},{11... | collective-permute-start | bytes 110600 | tf_op jit(solution)/shard_map/ppermute | solution.py:27
  30.1 4.0 copy-start.1
  45.2 169.3 %slice-start.2 = ((f32[3,16,64,128]{3,2,1,0:T(8,128)}), f32[3,1,64,128]{3,2,1,0:T(8,128)S(1)}, s32[]{:S(2)}) async-start(f32[3,16,64,128]{3,2,1,0:T(8,128)} %param.31), calls=%async_computation.5 | async-start | bytes 196608 | tf_op jit(solution)/shard_map/slice | solution.py:170
  214.5 23.4 %copy-start.43 = (f32[16,64,128]{2,1,0:T(8,128)S(1)}, f32[16,64,128]{2,1,0:T(8,128)}, u32[]{:S(2)}) copy-start(f32[16,64,128]{2,1,0:T(8,128)} %get-tuple-element.403) | copy-start | bytes 1572868
  234.5 8.2 %copy-start.62 = (s32[16,1024]{1,0:T(8,128)}, s32[16,1024]{1,0:T(8,128)S(1)}, u32[]{:S(2)}) copy-start(s32[16,1024]{1,0:T(8,128)S(1)} %get-tuple-element.902) | copy-start | bytes 196612
  234.5 8.2 %copy-start.63 = (s32[16,1024]{1,0:T(8,128)}, s32[16,1024]{1,0:T(8,128)S(1)}, u32[]{:S(2)}) copy-start(s32[16,1024]{1,0:T(8,128)S(1)} %get-tuple-element.904) | copy-start | bytes 196612
  234.5 7.0 %copy-start.44 = (f32[16,64,128]{2,1,0:T(8,128)S(1)}, f32[16,64,128]{2,1,0:T(8,128)}, u32[]{:S(2)}) copy-start(f32[16,64,128]{2,1,0:T(8,128)} %get-tuple-element.401) | copy-start | bytes 1572868
  234.5 7.0 %copy-start.45 = (f32[16,64,128]{2,1,0:T(8,128)S(1)}, f32[16,64,128]{2,1,0:T(8,128)}, u32[]{:S(2)}) copy-start(f32[16,64,128]{2,1,0:T(8,128)} %get-tuple-element.402) | copy-start | bytes 1572868
  234.5 8.2 %copy-start.55 = (f32[3,8,64,128]{3,2,1,0:T(8,128)S(1)}, f32[3,8,64,128]{3,2,1,0:T(8,128)}, u32[]{:S(2)}) copy-start(f32[3,8,64,128]{3,2,1,0:T(8,128)} %param.34) | copy-start | bytes 2359300
  234.5 8.2 %copy-start.65 = (f32[3]{0:T(128)S(1)}, f32[3]{0:T(128)}, u32[]{:S(2)}) copy-start(f32[3]{0:T(128)} %get-tuple-element.265) | copy-start | bytes 40
  234.5 8.2 %copy-start.66 = (f32[3]{0:T(128)S(1)}, f32[3]{0:T(128)}, u32[]{:S(2)}) copy-start(f32[3]{0:T(128)} %get-tuple-element.266) | copy-start | bytes 40
  234.5 8.2 %copy-start.67 = (f32[3]{0:T(128)S(1)}, f32[3]{0:T(128)}, u32[]{:S(2)}) copy-start(f32[3]{0:T(128)} %get-tuple-element.267) | copy-start | bytes 40
  234.5 8.2 %copy-start.68 = (f32[3]{0:T(128)S(1)}, f32[3]{0:T(128)}, u32[]{:S(2)}) copy-start(f32[3]{0:T(128)} %get-tuple-element.268) | copy-start | bytes 40
  234.5 8.2 %copy-start.69 = (f32[3]{0:T(128)S(1)}, f32[3]{0:T(128)}, u32[]{:S(2)}) copy-start(f32[3]{0:T(128)} %get-tuple-element.269) | copy-start | bytes 40
  244.0 16.3 %copy-start.24 = (f32[3,8,64,128]{3,2,1,0:T(8,128)}, f32[3,8,64,128]{3,2,1,0:T(8,128)S(1)}, u32[]{:S(2)}) copy-start(f32[3,8,64,128]{3,2,1,0:T(8,128)S(1)} %get-tuple-element.456) | copy-start | bytes 2359300
  298.4 10.8 %all-to-all-start.1 = ((f32[3,8,2048]{2,0,1:T(4,128)}), f32[3,8,2048]{2,0,1:T(4,128)S(1)}, u32[]{:S(2)}, u32[]{:S(2)}) async-start(f32[3,8,2048]{2,0,1:T(4,128)} %copy.166), calls=%async_computation.1 | async-start | bytes 524288 | tf_op jit(solution)/shard_map/all_to_all | solution.py:160
  309.9 43.3 %all-to-all-start = ((f32[3,8,2048]{2,0,1:T(4,128)}), f32[3,8,2048]{2,0,1:T(4,128)S(1)}, u32[]{:S(2)}, u32[]{:S(2)}) async-start(f32[3,8,2048]{2,0,1:T(4,128)} %copy.163), calls=%async_computation | async-start | bytes 524288 | tf_op jit(solution)/shard_map/all_to_all | solution.py:160
  354.1 35.9 %copy-start.58 = (f32[8,3,1024]{2,1,0:T(4,128)S(1)}, f32[8,3,1024]{2,1,0:T(4,128)}, u32[]{:S(2)}) copy-start(f32[8,3,1024]{2,1,0:T(4,128)} %copy-done.57) | copy-start | bytes 294916
  390.0 8.7 %copy-start.16 = (f32[1,1,64,128,128]{4,3,2,1,0:T(8,128)S(1)}, f32[1,1,64,128,128]{4,3,2,1,0:T(8,128)}, u32[]{:S(2)}) copy-start(f32[1,1,64,128,128]{4,3,2,1,0:T(8,128)} %param.40) | copy-start | bytes 12582916
  390.0 8.7 %copy-start.60 = (f32[64,128]{1,0:T(8,128)S(1)}, f32[64,128]{1,0:T(8,128)}, u32[]{:S(2)}) copy-start(f32[64,128]{1,0:T(8,128)} %fusion.319) | copy-start | bytes 98308
  423.6 24.1 %collective-permute-start.7 = (f32[3,24,64,2]{2,1,3,0:T(8,128)}, f32[3,24,64,2]{2,1,3,0:T(8,128)}, u32[]{:S(2)}, u32[]{:S(2)}) collective-permute-start(f32[3,24,64,2]{2,1,3,0:T(8,128)} %copy.174), channel_id=1, source_target_pairs={{1,0},{2,1},{3,2},{4,3},{5,4},{6,5},{7,6},{9,8},{10,9},{11,10},{12... | collective-permute-start | bytes 110600 | tf_op jit(solution)/shard_map/ppermute | solution.py:28
  426.4 18.2 %collective-permute-start.6 = (f32[3,24,64,2]{2,1,3,0:T(8,128)}, f32[3,24,64,2]{2,1,3,0:T(8,128)}, u32[]{:S(2)}, u32[]{:S(2)}) collective-permute-start(f32[3,24,64,2]{2,1,3,0:T(8,128)} %copy.173), channel_id=1, source_target_pairs={{0,1},{1,2},{2,3},{3,4},{4,5},{5,6},{6,7},{8,9},{9,10},{10,11},{11... | collective-permute-start | bytes 110600 | tf_op jit(solution)/shard_map/ppermute | solution.py:27
  436.6 14.2 %copy-start.3 = (f32[3,24,64,128]{3,2,1,0:T(8,128)S(1)}, f32[3,24,64,128]{3,2,1,0:T(8,128)}, u32[]{:S(2)}) copy-start(f32[3,24,64,128]{3,2,1,0:T(8,128)} %copy-done.2) | copy-start | bytes 7077892
  436.6 19.0 %collective-permute-start.4 = (f32[3,24,2,128]{3,2,1,0:T(2,128)}, f32[3,24,2,128]{3,2,1,0:T(2,128)S(1)}, u32[]{:S(2)}, u32[]{:S(2)}) collective-permute-start(f32[3,24,2,128]{3,2,1,0:T(2,128)} %get-tuple-element.436), channel_id=1, source_target_pairs={{0,8},{8,16},{16,24},{24,32},{32,40},{40,48},{48,56},{56,64},{64,7... | collective-permute-start | bytes 221192 | tf_op jit(solution)/shard_map/ppermute | solution.py:27
  438.7 17.0 %collective-permute-start.5 = (f32[3,24,2,128]{3,2,1,0:T(2,128)}, f32[3,24,2,128]{3,2,1,0:T(2,128)S(1)}, u32[]{:S(2)}, u32[]{:S(2)}) collective-permute-start(f32[3,24,2,128]{3,2,1,0:T(2,128)} %get-tuple-element.437), channel_id=1, source_target_pairs={{8,0},{16,8},{24,16},{32,24},{40,32},{48,40},{56,48},{64,56},{72,6... | collective-permute-start | bytes 221192 | tf_op jit(solution)/shard_map/ppermute | solution.py:28
  458.0 3.2 copy-start.36
  461.2 3.1 copy-start.26
  464.1 3.7 copy-start.18
  464.1 15.6 %copy-start.9 = (f32[24,64,128]{2,1,0:T(8,128)}, f32[24,64,128]{2,1,0:T(8,128)S(1)}, u32[]{:S(2)}) copy-start(f32[24,64,128]{2,1,0:T(8,128)S(1)} %get-tuple-element.378) | copy-start | bytes 2359300
  464.1 15.6 %copy-start.21 = (f32[24,64,128]{2,1,0:T(8,128)}, f32[24,64,128]{2,1,0:T(8,128)S(1)}, u32[]{:S(2)}) copy-start(f32[24,64,128]{2,1,0:T(8,128)S(1)} %get-tuple-element.377) | copy-start | bytes 2359300
  466.9 11.0 %copy-start.11 = (f32[24,64,128]{2,1,0:T(8,128)}, f32[24,64,128]{2,1,0:T(8,128)S(1)}, u32[]{:S(2)}) copy-start(f32[24,64,128]{2,1,0:T(8,128)S(1)} %get-tuple-element.379) | copy-start | bytes 2359300
  467.0 12.8 %copy-start.6 = (f32[24,64,128]{2,1,0:T(8,128)}, f32[24,64,128]{2,1,0:T(8,128)S(1)}, u32[]{:S(2)}) copy-start(f32[24,64,128]{2,1,0:T(8,128)S(1)} %get-tuple-element.380) | copy-start | bytes 2359300
  468.5 44.1 %collective-permute-start.8 = (f32[3,24,2,128]{3,2,1,0:T(2,128)}, f32[3,24,2,128]{3,2,1,0:T(2,128)}, u32[]{:S(2)}, u32[]{:S(2)}) collective-permute-start(f32[3,24,2,128]{3,2,1,0:T(2,128)} %get-tuple-element.426), channel_id=1, source_target_pairs={{0,8},{8,16},{16,24},{24,32},{32,40},{40,48},{48,56},{56,64},{64,7... | collective-permute-start | bytes 221192 | tf_op jit(solution)/shard_map/ppermute | solution.py:27
  470.5 42.2 %collective-permute-start.9 = (f32[3,24,2,128]{3,2,1,0:T(2,128)}, f32[3,24,2,128]{3,2,1,0:T(2,128)}, u32[]{:S(2)}, u32[]{:S(2)}) collective-permute-start(f32[3,24,2,128]{3,2,1,0:T(2,128)} %get-tuple-element.427), channel_id=1, source_target_pairs={{8,0},{16,8},{24,16},{32,24},{40,32},{48,40},{56,48},{64,56},{72,6... | collective-permute-start | bytes 221192 | tf_op jit(solution)/shard_map/ppermute | solution.py:28
  489.1 15.0 %collective-permute-start.11 = (f32[3,24,64,2]{2,1,3,0:T(8,128)}, f32[3,24,64,2]{2,1,3,0:T(8,128)}, u32[]{:S(2)}, u32[]{:S(2)}) collective-permute-start(f32[3,24,64,2]{2,1,3,0:T(8,128)} %copy.185), channel_id=1, source_target_pairs={{1,0},{2,1},{3,2},{4,3},{5,4},{6,5},{7,6},{9,8},{10,9},{11,10},{12... | collective-permute-start | bytes 110600 | tf_op jit(solution)/shard_map/ppermute | solution.py:28
  491.1 10.0 %collective-permute-start.10 = (f32[3,24,64,2]{2,1,3,0:T(8,128)}, f32[3,24,64,2]{2,1,3,0:T(8,128)}, u32[]{:S(2)}, u32[]{:S(2)}) collective-permute-start(f32[3,24,64,2]{2,1,3,0:T(8,128)} %copy.184), channel_id=1, source_target_pairs={{0,1},{1,2},{2,3},{3,4},{4,5},{5,6},{6,7},{8,9},{9,10},{10,11},{11... | collective-permute-start | bytes 110600 | tf_op jit(solution)/shard_map/ppermute | solution.py:27
  520.6 35.2 %copy-start.56 = (f32[8,2048]{1,0:T(8,128)S(1)}, f32[8,2048]{1,0:T(8,128)}, u32[]{:S(2)}) copy-start(f32[8,2048]{1,0:T(8,128)} %fusion.317) | copy-start | bytes 196612
  606.4 8.6 %copy-start.17 = (f32[1,1,64,128,128]{4,3,2,1,0:T(8,128)S(1)}, f32[1,1,64,128,128]{4,3,2,1,0:T(8,128)}, u32[]{:S(2)}) copy-start(f32[1,1,64,128,128]{4,3,2,1,0:T(8,128)} %param.40) | copy-start | bytes 12582916
  615.1 6.6 copy-start.61
  634.7 23.3 %collective-permute-start.15 = (f32[3,24,64,2]{2,1,3,0:T(8,128)S(1)}, f32[3,24,64,2]{2,1,3,0:T(8,128)S(1)}, u32[]{:S(2)}, u32[]{:S(2)}) collective-permute-start(f32[3,24,64,2]{2,1,3,0:T(8,128)S(1)} %copy.195), channel_id=1, source_target_pairs={{1,0},{2,1},{3,2},{4,3},{5,4},{6,5},{7,6},{9,8},{10,9},{11,10},{12... | collective-permute-start | bytes 110600 | tf_op jit(solution)/shard_map/ppermute | solution.py:28
  637.2 17.7 %collective-permute-start.14 = (f32[3,24,64,2]{2,1,3,0:T(8,128)}, f32[3,24,64,2]{2,1,3,0:T(8,128)}, u32[]{:S(2)}, u32[]{:S(2)}) collective-permute-start(f32[3,24,64,2]{2,1,3,0:T(8,128)} %copy.194), channel_id=1, source_target_pairs={{0,1},{1,2},{2,3},{3,4},{4,5},{5,6},{6,7},{8,9},{9,10},{10,11},{11... | collective-permute-start | bytes 110600 | tf_op jit(solution)/shard_map/ppermute | solution.py:27
  647.0 17.9 %collective-permute-start.12 = (f32[3,24,2,128]{3,2,1,0:T(2,128)}, f32[3,24,2,128]{3,2,1,0:T(2,128)}, u32[]{:S(2)}, u32[]{:S(2)}) collective-permute-start(f32[3,24,2,128]{3,2,1,0:T(2,128)} %get-tuple-element.424), channel_id=1, source_target_pairs={{0,8},{8,16},{16,24},{24,32},{32,40},{40,48},{48,56},{56,64},{64,7... | collective-permute-start | bytes 221192 | tf_op jit(solution)/shard_map/ppermute | solution.py:27
  648.9 16.0 %collective-permute-start.13 = (f32[3,24,2,128]{3,2,1,0:T(2,128)}, f32[3,24,2,128]{3,2,1,0:T(2,128)}, u32[]{:S(2)}, u32[]{:S(2)}) collective-permute-start(f32[3,24,2,128]{3,2,1,0:T(2,128)} %get-tuple-element.425), channel_id=1, source_target_pairs={{8,0},{16,8},{24,16},{32,24},{40,32},{48,40},{56,48},{64,56},{72,6... | collective-permute-start | bytes 221192 | tf_op jit(solution)/shard_map/ppermute | solution.py:28
  (43 other events, 66.4 us)
where the time goes:
time: 689 us; the launch traced here: 678 us
  local copies, waits for them, and re-layouts  243 us (35%)
  other arithmetic  191 us (28%)
  matrix products  141 us (20%)
  starting transfers between devices  79.8 us (12%)
  blocking collectives  13.7 us (2%)
    dot_general x72, matrix products, one_block(): spread = jnp.dot(flattened, lane_onehot, precision=lax.Precision.HIGHEST)  111 us
    reduce_sum x64, other arithmetic, slot_cells(): return jnp.sum(jnp.where(matched, owner_cells[None, :], 0), axis=1)  69.1 us
    dynamic_slice x72, local copies, waits for them, and re-layouts, select_cells(): lax.map(one_block, (lane_index.reshape(-1, width_block), group_index.resh...  44.3 us
    dynamic_slice x64, local copies, waits for them, and re-layouts, owner_slots(): return lax.map(slot_cells, first_slots).reshape(CAP)  37.1 us
    ppermute x8, starting transfers between devices, extended(): before = lax.ppermute(last, axis, up)  36.2 us
    add x64, other arithmetic, slot_cells(): slot_ids = first_slot + lax.broadcasted_iota(jnp.int32, (slot_block, 1), 0)  35.8 us
    ppermute x8, starting transfers between devices, extended(): after = lax.ppermute(first, axis, down)  33.3 us
    slice x11, local copies, waits for them, and re-layouts, extended(): last = lax.slice_in_dim(value, length - width, length, axis=dim)  27.8 us
  transfers between devices with their start and end apart: 18, of which 1 were waited for; matrix products, arithmetic and copies ran while one was open for 49% of the time, Pallas kernels for 0%

commit v1 on v0

v1 whole, which is shorter than its diff:
```python
import functools

import jax
import jax.numpy as jnp
from jax import lax
from jax.experimental import pallas as pl
from jax.experimental.pallas import tpu as pltpu
from jax.sharding import PartitionSpec as P

NZ = 16
BZ = 8
CX = 64
CY = 128
ZR = 8
ZONES = 8
GROUPS = 64
BLK = 128
DT = 0.12
NEAR = 9.0 / 8.0
FAR = 1.0 / 24.0

VM = pl.BlockSpec(memory_space=pltpu.VMEM)
SM = pl.BlockSpec(memory_space=pltpu.SMEM)
PARAMS = pltpu.CompilerParams(vmem_limit_bytes=20 * 2**20)
F32 = jnp.float32
BF16 = jnp.bfloat16
XS = (0, 1, 2)
YS = (2, 3, 4)
VS = (0, 1, 2)


def sds(shape, dtype=F32):
    return jax.ShapeDtypeStruct(shape, dtype)


def lanes():
    return lax.broadcasted_iota(jnp.int32, (CX, CY), 1)


def slot(k0, layers, c):
    first = k0 + c * layers
    return first // 32, first % 32


def put_x(xlo_ref, xhi_ref, k, value):
    xlo_ref[k] = value[0:2]
    xhi_ref[k] = value[CX - 2 : CX]


def put_y(q_ref, j, m, value):
    moved = pltpu.roll(value, 2 + 4 * m, 1)
    q_ref[j] = jnp.where(lanes() // 4 == m, moved, q_ref[j])


def y_halo(qm_ref, j, m):
    return pltpu.roll(qm_ref[j], CY - 2 - 4 * m, 1)


def merge_q(flags_ref, ql_ref, qr_ref, qm_ref):
    part = lanes() % 4
    for j in range(ql_ref.shape[0]):
        left = jnp.where(flags_ref[2] > 0, ql_ref[j], 0.0)
        right = jnp.where(flags_ref[3] > 0, qr_ref[j], 0.0)
        qm_ref[j] = jnp.where(part < 2, left, right)


def fill_pad(flags_ref, src_ref, comps, xb_ref, xa_ref, k0, pad_ref, layers):
    def body(z, _):
        for i, c in enumerate(comps):
            k = k0 + i * layers + z
            pad_ref[i, z, 8 : 8 + CX] = src_ref[c, z]
            pad_ref[i, z, 6:8] = jnp.where(flags_ref[0] > 0, xb_ref[k], 0.0)
            pad_ref[i, z, 8 + CX : 10 + CX] = jnp.where(flags_ref[1] > 0, xa_ref[k], 0.0)
        return 0

    lax.fori_loop(0, layers, body, 0)


def dx(pad_ref, i, z, forward):
    def at(d):
        return pad_ref[i, z, 8 + d : 8 + d + CX]

    if forward:
        return NEAR * (at(1) - at(0)) - FAR * (at(2) - at(-1))
    return NEAR * (at(0) - at(-1)) - FAR * (at(1) - at(-2))


def dy(value, halo, forward):
    lane = lanes()
    before = pltpu.roll(jnp.where(lane >= CY - 1, halo, value), 1, 1)
    after = pltpu.roll(jnp.where(lane < 1, halo, value), CY - 1, 1)
    if forward:
        return NEAR * (after - value) - FAR * (pltpu.roll(jnp.where(lane < 2, halo, value), CY - 2, 1) - before)
    return NEAR * (value - before) - FAR * (after - pltpu.roll(jnp.where(lane >= CY - 2, halo, value), 2, 1))


def dz(src_ref, c, z, layers, forward, edge):
    def at(d):
        if edge and not 0 <= z + d < layers:
            return jnp.zeros((CX, CY), F32)
        return src_ref[c, z + d]

    if forward:
        return NEAR * (at(1) - at(0)) - FAR * (at(2) - at(-1))
    return NEAR * (at(0) - at(-1)) - FAR * (at(1) - at(-2))


def over_layers(layers, body):
    for z in (0, 1):
        body(z, True)

    def inner(z, _):
        body(z, False)
        return 0

    lax.fori_loop(2, layers - 2, inner, 0)
    for z in (layers - 2, layers - 1):
        body(z, True)


def pack_kernel(zm_ref, sb_ref, sx_ref, ids_ref, xlo_ref, xhi_ref, q_ref, med_ref):
    q_ref[...] = jnp.zeros(q_ref.shape, F32)
    for ref, layers, k0 in ((sb_ref, NZ, 0), (sx_ref, BZ, 3 * NZ)):

        def body(z, _, ref=ref, layers=layers, k0=k0):
            for i, c in enumerate(XS):
                put_x(xlo_ref, xhi_ref, k0 + i * layers + z, ref[c, z])
            for i, c in enumerate(YS):
                j, m = slot(k0, layers, i)
                put_y(q_ref, j, m + z, ref[c, z])
            return 0

        lax.fori_loop(0, layers, body, 0)

    def media(z, _):
        ids = ids_ref[z]
        for c in range(3):
            value = jnp.full((CX, CY), zm_ref[c, 0], F32)
            for n in range(1, ZONES):
                value = jnp.where(ids == n, zm_ref[c, n], value)
            med_ref[c, z] = value
        return 0

    lax.fori_loop(0, BZ, media, 0)


def start_edges(carried, xlo_ref, xhi_ref, q_ref):
    q_ref[...] = jnp.zeros(q_ref.shape, F32)
    if not carried:
        return 0
    done = carried[0].shape[0]
    xlo_ref[0:done] = carried[0][...]
    xhi_ref[0:done] = carried[1][...]
    q_ref[0 : carried[2].shape[0]] = carried[2][...]
    return done


def vel_kernel(layers, k0, forced, carry, *refs):
    flags_ref, v_ref, s_ref, med_ref, xb_ref, xa_ref, ql_ref, qr_ref = refs[:8]
    refs = refs[8:]
    if forced:
        force_ref, refs = refs[0], refs[1:]
    carried, refs = (refs[:3], refs[3:]) if carry else ((), refs)
    out_ref, xlo_ref, xhi_ref, q_ref, pad_ref, qm_ref = refs
    fill_pad(flags_ref, s_ref, XS, xb_ref, xa_ref, k0, pad_ref, layers)
    merge_q(flags_ref, ql_ref, qr_ref, qm_ref)
    o0 = start_edges(carried, xlo_ref, xhi_ref, q_ref)

    def body(z, edge):
        def ydiff(i, forward):
            j, m = slot(k0, layers, i)
            return dy(s_ref[YS[i], z], y_halo(qm_ref, j, m + z), forward)

        scale = DT * med_ref[2, z]
        sums = (
            dx(pad_ref, 0, z, True) + ydiff(0, False) + dz(s_ref, 1, z, layers, False, edge),
            dx(pad_ref, 2, z, False) + ydiff(2, True) + dz(s_ref, 3, z, layers, False, edge),
            dx(pad_ref, 1, z, False) + ydiff(1, False) + dz(s_ref, 5, z, layers, True, edge),
        )
        for c in VS:
            new = v_ref[c, z] + scale * sums[c]
            if forced and edge and z == layers - 1:
                new = new + scale * force_ref[c]
            out_ref[c, z] = new
            put_x(xlo_ref, xhi_ref, o0 + c * layers + z, new)
            j, m = slot(o0, layers, c)
            put_y(q_ref, j, m + z, new)

    over_layers(layers, body)


def stress_kernel(layers, k0, edges, *refs):
    flags_ref, v_ref, s_ref, med_ref, xb_ref, xa_ref, ql_ref, qr_ref, out_ref = refs[:9]
    refs = refs[9:]
    if edges:
        xlo_ref, xhi_ref, q_ref = refs[:3]
        refs = refs[3:]
        q_ref[...] = jnp.zeros(q_ref.shape, F32)
    pad_ref, qm_ref = refs
    fill_pad(flags_ref, v_ref, VS, xb_ref, xa_ref, k0, pad_ref, layers)
    merge_q(flags_ref, ql_ref, qr_ref, qm_ref)

    def body(z, edge):
        def halo(c):
            j, m = slot(k0, layers, c)
            return y_halo(qm_ref, j, m + z)

        lam, mu = DT * med_ref[0, z], DT * med_ref[1, z]
        mod = lam + 2.0 * mu
        hx, hy, hz = halo(0), halo(1), halo(2)
        ex = dx(pad_ref, 0, z, False)
        ey = dy(v_ref[1, z], hy, False)
        ez = dz(v_ref, 2, z, layers, False, edge)
        new = (
            s_ref[0, z] + (mod * ex + lam * (ey + ez)),
            s_ref[1, z] + mu * (dz(v_ref, 0, z, layers, True, edge) + dx(pad_ref, 2, z, True)),
            s_ref[2, z] + mu * (dy(v_ref[0, z], hx, True) + dx(pad_ref, 1, z, True)),
            s_ref[3, z] + mu * (dz(v_ref, 1, z, layers, True, edge) + dy(v_ref[2, z], hz, True)),
            s_ref[4, z] + (mod * ey + lam * (ex + ez)),
            s_ref[5, z] + (mod * ez + lam * (ex + ey)),
        )
        for c in range(6):
            out_ref[c, z] = new[c]
        if edges:
            for i, c in enumerate(XS):
                put_x(xlo_ref, xhi_ref, i * layers + z, new[c])
            for i, c in enumerate(YS):
                j, m = slot(0, layers, i)
                put_y(q_ref, j, m + z, new[c])

    over_layers(layers, body)


def row_lookup(idx_row):
    return jnp.broadcast_to(idx_row, (8, CY))


def take(table, index):
    return jnp.take_along_axis(table, index, axis=1, mode="promise_in_bounds")


def select_sorted(lo_ref, hi_ref, rs_ref, ys_ref, v_ref, sorted_ref):
    sub = lax.broadcasted_iota(jnp.int32, (8, CY), 0)
    top = v_ref.shape[0] * 8 - 1
    comps = v_ref.shape[1]
    several = 12 // comps

    def part(k, rows, index, accs):
        t, x = k // 8, pl.multiple_of(k % 8 * 8, 8)
        hit = rows == 8 * k
        return tuple(jnp.where(hit, take(v_ref[t, c, pl.ds(x, 8), :], index), accs[c]) for c in range(comps))

    def body(b, _):
        state = []
        for u in range(several):
            g = b * several + u
            index = row_lookup(ys_ref[pl.ds(g, 1), :])
            rows = row_lookup(rs_ref[pl.ds(g, 1), :]) - sub
            accs = (jnp.zeros((8, CY), F32),) * comps
            first = lo_ref[g]
            for d in range(2):
                accs = part(jnp.minimum(first + d, top), rows, index, accs)
            state.append((g, index, rows, first, accs))
        for g, index, rows, first, accs in state:
            accs = lax.fori_loop(
                first + 2, hi_ref[g] + 1, lambda k, a, r=rows, i=index: part(k, r, i, a), accs
            )
            for c in range(comps):
                sorted_ref[c, pl.ds(g, 1), :] = jnp.sum(accs[c], axis=0, keepdims=True)
        return 0

    lax.fori_loop(0, GROUPS // several, body, 0)


def unsort(sorted_ref, inv_ref, g):
    sub = lax.broadcasted_iota(jnp.int32, (8, CY), 0)
    place = row_lookup(inv_ref[pl.ds(g, 1), :])
    index = place & (CY - 1)
    rows = (place >> 7) - sub
    comps = sorted_ref.shape[0]
    accs = [jnp.zeros((8, CY), F32)] * comps
    for k in range(GROUPS // 8):
        hit = rows == 8 * k
        for c in range(comps):
            accs[c] = jnp.where(hit, take(sorted_ref[c, 8 * k : 8 * k + 8, :], index), accs[c])
    tiles = []
    for f in range(0, comps, 3):
        tile = jnp.zeros((8, CY), F32)
        for c in range(3):
            tile = jnp.where(sub == c, jnp.sum(accs[f + c], axis=0, keepdims=True), tile)
        tiles.append(tile)
    return tiles


def force_kernel(first, *refs):
    lo_ref, hi_ref, rs_ref, ys_ref, inv_ref, v_ref, stiff_ref, mass_ref = refs[:8]
    refs = refs[8:]
    if not first:
        prev_ref, refs = refs[0], refs[1:]
    force_ref, refs = refs[0], refs[1:]
    if first:
        cur_ref, refs = refs[0], refs[1:]
    (sorted_ref,) = refs
    select_sorted(lo_ref, hi_ref, rs_ref, ys_ref, v_ref, sorted_ref)
    several = 4

    def body(b, _):
        for u in range(several):
            g = b * several + u
            tiles = unsort(sorted_ref, inv_ref, g)
            tile = tiles[-1]
            if first:
                cur_ref[g] = tile
            change = (tile - (tiles[0] if first else prev_ref[g])) / DT
            both = jnp.concatenate([tile, change], axis=1)
            high = both.astype(BF16)
            low = (both - high.astype(F32)).astype(BF16)
            matrix = jnp.concatenate([stiff_ref[g], mass_ref[g]], axis=1)
            matrix_high = matrix.astype(BF16)
            matrix_low = (matrix - matrix_high.astype(F32)).astype(BF16)
            stacked = jnp.concatenate([high, low], axis=0)
            weights = jnp.concatenate([matrix_high, matrix_low], axis=0)
            product = lax.dot_general(stacked, weights, (((1,), (1,)), ((), ())), preferred_element_type=F32)
            total = product[0:8, 0:BLK] + (product[0:8, BLK:] + product[8:16, 0:BLK])
            for c in range(3):
                force_ref[c, pl.ds(g, 1), :] = -total[c : c + 1]
        return 0

    lax.fori_loop(0, GROUPS // several, body, 0)


def ring(value, axis, step):
    n = lax.axis_size(axis)
    return lax.ppermute(value, axis, [(i, (i + step) % n) for i in range(n)])


def trade(edges):
    xlo, xhi, q = edges
    return ring(xhi, "gx", 1), ring(xlo, "gx", -1), ring(q, "gy", 1), ring(q, "gy", -1)


def cost(flops, size):
    return pl.CostEstimate(flops=flops, bytes_accessed=size, transcendentals=0)


def edge_shapes(layers):
    k = 3 * layers
    return (sds((k, 2, CY)), sds((k, 2, CY)), sds((-(-k // 32), CX, CY)))


def velocity_step(name, flags, v, s, media, halos, k0, force=None, carry=()):
    layers = v.shape[1]
    out = pl.pallas_call(
        functools.partial(vel_kernel, layers, k0, force is not None, bool(carry)),
        out_shape=(sds(v.shape), *edge_shapes(layers + (carry[0].shape[0] // 3 if carry else 0))),
        in_specs=[SM] + [VM] * (7 + (force is not None) + len(carry)),
        out_specs=(VM,) * 4,
        scratch_shapes=[pltpu.VMEM((3, layers, CX + 16, CY), F32), pltpu.VMEM(halos[2].shape, F32)],
        compiler_params=PARAMS,
        name=name,
        cost_estimate=cost(60 * v.size, 16 * v.size),
    )(flags, v, s, media, *halos, *(() if force is None else (force,)), *carry)
    return out[0], out[1:]


def stress_step(name, flags, v, s, media, halos, k0, edges):
    layers = v.shape[1]
    out = pl.pallas_call(
        functools.partial(stress_kernel, layers, k0, edges),
        out_shape=(sds(s.shape), *(edge_shapes(layers) if edges else ())),
        in_specs=[SM] + [VM] * 7,
        out_specs=(VM,) * (4 if edges else 1),
        scratch_shapes=[pltpu.VMEM((3, layers, CX + 16, CY), F32), pltpu.VMEM(halos[2].shape, F32)],
        compiler_params=PARAMS,
        name=name,
        cost_estimate=cost(60 * v.size, 16 * v.size),
    )(flags, v, s, media, *halos)
    return out[0], out[1:]


def shards(
    basin_v, basin_s, basin_media, box_v, box_s, zone_ids, zone_media, corridor_tile, corridor_cell, drm_stiff, drm_mass
):
    gx, gy = lax.axis_index("gx"), lax.axis_index("gy")
    nx, ny = lax.axis_size("gx"), lax.axis_size("gy")
    flags = jnp.stack([gx > 0, gx < nx - 1, gy > 0, gy < ny - 1]).astype(jnp.int32)

    def spread(layer):
        return lax.all_to_all(jnp.broadcast_to(layer[None], (ny, *layer.shape)), "gy", 0, 0, tiled=True)

    *edges, box_media = pl.pallas_call(
        pack_kernel,
        out_shape=(*edge_shapes(NZ + BZ), sds((3, BZ, CX, CY))),
        in_specs=[SM, VM, VM, VM],
        out_specs=(VM,) * 4,
        compiler_params=PARAMS,
        name="pack",
        cost_estimate=cost(2**20, 2**22),
    )(zone_media, basin_s, box_s, zone_ids)
    halos = trade(edges)

    own_tile = lax.dynamic_index_in_dim(corridor_tile[0, :, :, 0], gy, 0, keepdims=False)
    own_cell = lax.dynamic_index_in_dim(corridor_cell[0], gy, 0, keepdims=False)
    requests = lax.iota(jnp.int32, GROUPS * BLK)
    keys = lax.sort((own_tile * (CX * CY) + own_cell) * (GROUPS * BLK) + requests)
    rows = (keys >> 20).reshape(GROUPS, BLK)
    cols = ((keys >> 13) & (CY - 1)).reshape(GROUPS, BLK)
    inverse = lax.sort(((keys & 8191) << 13) | requests)
    inverse = (inverse & 8191).reshape(GROUPS, BLK)
    first, last = rows[:, 0] >> 3, rows[:, BLK - 1] >> 3
    lookup = (first, last, rows, cols, inverse)

    def forces(name, layers, previous):
        first = previous is None
        comps = layers.shape[1]
        shapes = (sds((3, CX, CY)), sds((GROUPS, 8, BLK)))
        return pl.pallas_call(
            functools.partial(force_kernel, first),
            out_shape=shapes if first else shapes[:1],
            in_specs=[SM, SM] + [VM] * (6 if first else 7),
            out_specs=(VM, VM) if first else (VM,),
            scratch_shapes=[pltpu.VMEM((comps, GROUPS, BLK), F32)],
            compiler_params=PARAMS,
            name=name,
            cost_estimate=cost(2**30, 2**23),
        )(*lookup, layers, drm_stiff[0, 0], drm_mass[0, 0], *(() if first else (previous,)))

    layer0 = basin_v[:, ZR]
    basin_v, edges_b = velocity_step("basin_v1", flags, basin_v, basin_s, basin_media, halos, 0)
    layers01 = spread(jnp.concatenate([layer0, basin_v[:, ZR]]))
    halos_b = trade(edges_b)
    basin_s, edges_b = stress_step("basin_s1", flags, basin_v, basin_s, basin_media, halos_b, 0, True)
    force, current = forces("force1", layers01, None)
    box_v, edges = velocity_step("box_v1", flags, box_v, box_s, box_media, halos, 3 * NZ, force, edges_b)
    halos = trade(edges)
    basin_v, edges_b = velocity_step("basin_v2", flags, basin_v, basin_s, basin_media, halos, 0)
    layer2 = spread(basin_v[:, ZR])
    box_s, edges_x = stress_step("box_s1", flags, box_v, box_s, box_media, halos, 3 * NZ, True)
    halos_x = trade(edges_x)
    (force,) = forces("force2", layer2, current)
    box_v, edges = velocity_step("box_v2", flags, box_v, box_s, box_media, halos_x, 0, force, edges_b)
    halos = trade(edges)
    basin_s, _ = stress_step("basin_s2", flags, basin_v, basin_s, basin_media, halos, 0, False)
    box_s, _ = stress_step("box_s2", flags, box_v, box_s, box_media, halos, 3 * NZ, False)
    return basin_v, basin_s, box_v, box_s


def solution(mesh):
    field = P(None, None, "gx", "gy")
    return jax.shard_map(
        shards,
        mesh=mesh,
        in_specs=(
            field,
            field,
            field,
            field,
            field,
            P(None, "gx", "gy"),
            P(),
            P("gx", None, None, None),
            P("gx", None, None),
            P("gx", "gy", None, None, None),
            P("gx", "gy", None, None, None),
        ),
        out_specs=(field,) * 4,
        check_vma=False,
    )
```

time: 689 us -> 204 us (0.30)
  the two profiles are of different devices: /device:TPU:26 before, /device:TPU:0 now
where the time goes in v1:
time: 204 us; the launch traced here: 202 us
  Pallas kernels  67.9 us (33%)
  starting transfers between devices  55.7 us (27%)
  local copies, waits for them, and re-layouts  41.3 us (20%)
  other arithmetic  19.5 us (10%)
  waiting for transfers between devices  16.6 us (8%)
    ppermute x20, starting transfers between devices, ring(): return lax.ppermute(value, axis, [(i, (i + step) % n) for i in range(n)])  45.1 us
    unnamed x120, local copies, waits for them, and re-layouts  37.5 us
    pallas_call x2, Pallas kernels, forces(): pl.pallas_call(functools.partial(force_kernel, first), out_shape=shapes i...  25.8 us
    pallas_call x4, Pallas kernels, velocity_step(): pl.pallas_call(functools.partial(vel_kernel, layers, k0, force is not Non...  19.6 us
    pallas_call x4, Pallas kernels, stress_step(): pl.pallas_call(functools.partial(stress_kernel, layers, k0, edges), out_s...  18.7 us
    ppermute x20, waiting for transfers between devices, ring(): return lax.ppermute(value, axis, [(i, (i + step) % n) for i in range(n)])  16.6 us
    all_to_all x2, starting transfers between devices, spread(): lax.all_to_all(jnp.broadcast_to(layer[None], (ny, *layer.shape)), 'gy', 0...  10.6 us
    sort x1, other arithmetic, shards(): inverse = lax.sort((keys & 8191) << 13 | requests)  7.54 us
  transfers between devices with their start and end apart: 22, of which 8 were waited for; matrix products, arithmetic and copies ran while one was open for 10% of the time, Pallas kernels for 10%

profile of v1, /device:TPU:0, one launch (start us, length us, event | category | flops | bytes accessed | tf_op | source)
XLA Modules:
  0.0 202.1 jit_solution(8264170925849119507)
XLA Ops:
  0.7 1.9 copy-done.1
  2.6 1.4 copy-done.10
  5.6 3.9 %pack.1 = (f32[72,2,128]{2,1,0:T(2,128)}, f32[72,2,128]{2,1,0:T(2,128)}, f32[3,64,128]{2,1,0:T(8,128)}, f32[3,8,64,128]{3,2,1,0:T(8,128)S(1)}) custom-call(f32[3,8]{1,0:T(4,128)S(1)} %copy-done.56, f32[6,16,64,128]{3,2,1,0:T(8,128)S(1)} %copy-done.1, f32[6,8,64,128]{3,2,1,0:T(8,128)S(1)} %copy-done.10, s32[8,64,128]{2,1,0:T(8,128)S(1)} %copy-done.41), custom_call_target="tpu_custom_call" | custom-call | flops 1048576 | bytes 4194304 | tf_op jit(solution)/shard_map/pack/pallas_call | solution.py:391
  10.4 5.6 %collective-permute-start.3 = (f32[3,64,128]{2,1,0:T(8,128)}, f32[3,64,128]{2,1,0:T(8,128)S(1)}, u32[]{:S(2)}, u32[]{:S(2)}) collective-permute-start(f32[3,64,128]{2,1,0:T(8,128)} %get-tuple-element.40), channel_id=1, source_target_pairs={{0,7},{1,0},{2,1},{3,2},{4,3},{5,4},{6,5},{7,6},{8,15},{9,8},{10,9... | collective-permute-start | bytes 294920 | tf_op jit(solution)/shard_map/ppermute | solution.py:334
  15.9 3.9 %collective-permute-start.1 = (f32[72,2,128]{2,1,0:T(2,128)}, f32[72,2,128]{2,1,0:T(2,128)}, u32[]{:S(2)}, u32[]{:S(2)}) collective-permute-start(f32[72,2,128]{2,1,0:T(2,128)} %get-tuple-element.39), channel_id=1, source_target_pairs={{0,120},{8,0},{16,8},{24,16},{32,24},{40,32},{48,40},{56,48},{64,5... | collective-permute-start | bytes 221192 | tf_op jit(solution)/shard_map/ppermute | solution.py:334
  20.7 2.6 %collective-permute-done.refs_4_ = f32[72,2,128]{2,1,0:T(2,128)} collective-permute-done((f32[72,2,128]{2,1,0:T(2,128)}, f32[72,2,128]{2,1,0:T(2,128)}, u32[]{:S(2)}, u32[]{:S(2)}) %collective-permute-start) | collective-permute-done | bytes 73760 | tf_op jit(solution)/shard_map/ppermute | solution.py:334
  23.3 1.2 collective-permute-done.2.refs_6_
  24.5 1.4 copy-done.3
  25.9 1.4 copy-done.28
  27.3 5.8 %basin_v1.1 = (f32[3,16,64,128]{3,2,1,0:T(8,128)S(1)}, f32[48,2,128]{2,1,0:T(2,128)S(1)}, f32[48,2,128]{2,1,0:T(2,128)S(1)}, f32[2,64,128]{2,1,0:T(8,128)S(1)}) custom-call(s32[4]{0:T(128)S(1)} %add_convert_fusion.refs_0_, f32[3,16,64,128]{3,2,1,0:T(8,128)S(1)} %copy-done.28, f32[6,16,64,128]{3,2,1,0:T(8,128)S(1)} %copy-done.2, ...), custom_call_target="tpu_custom_call" | custom-call | flops 23592960 | bytes 6291456 | tf_op jit(solution)/shard_map/basin_v1/pallas_call | solution.py:353
  33.8 1.1 copy-done.19
  34.9 1.3 broadcast_in_dim.6
  36.3 5.7 %all-to-all-start = ((f32[8,6,64,128]{3,2,1,0:T(8,128)}), f32[8,6,64,128]{3,2,1,0:T(8,128)}, u32[]{:S(2)}, u32[]{:S(2)}) async-start(f32[8,6,64,128]{3,2,1,0:T(8,128)} %broadcast_in_dim.6), calls=%async_computation | async-start | bytes 3145728 | tf_op jit(solution)/shard_map/all_to_all | solution.py:389
  42.7 7.5 %sort.28 = (s32[8192]{0:T(1024)}, s32[8192]{0:T(1024)}) sort(s32[8192]{0:T(1024)} %iota_add_fusion, s32[8192]{0:T(1024)S(1)} %iota.12), dimensions={0}, to_apply=%region_0.1 | sort | flops 106496 | bytes 131072 | tf_op jit(solution)/shard_map/sort | solution.py:405
  50.2 1.4 iota_or_fusion
  52.2 7.5 %sort.29 = (s32[8192]{0:T(1024)}, s32[8192]{0:T(1024)}) sort(s32[8192]{0:T(1024)} %get-tuple-element.72, s32[8192]{0:T(1024)} %iota.14), dimensions={0}, to_apply=%region_1.2 | sort | flops 106496 | bytes 131072 | tf_op jit(solution)/shard_map/sort | solution.py:408
  59.7 1.4 and_bitcast_fusion.refs_4_
  61.1 5.6 %collective-permute-start.7 = (f32[2,64,128]{2,1,0:T(8,128)}, f32[2,64,128]{2,1,0:T(8,128)S(1)}, u32[]{:S(2)}, u32[]{:S(2)}) collective-permute-start(f32[2,64,128]{2,1,0:T(8,128)} %copy-done.57), channel_id=1, source_target_pairs={{0,7},{1,0},{2,1},{3,2},{4,3},{5,4},{6,5},{7,6},{8,15},{9,8},{10,9... | collective-permute-start | bytes 196616 | tf_op jit(solution)/shard_map/ppermute | solution.py:334
  66.7 3.9 %collective-permute-start.5 = (f32[48,2,128]{2,1,0:T(2,128)}, f32[48,2,128]{2,1,0:T(2,128)S(1)}, u32[]{:S(2)}, u32[]{:S(2)}) collective-permute-start(f32[48,2,128]{2,1,0:T(2,128)} %copy-done.58), channel_id=1, source_target_pairs={{0,120},{8,0},{16,8},{24,16},{32,24},{40,32},{48,40},{56,48},{64,5... | collective-permute-start | bytes 147464 | tf_op jit(solution)/shard_map/ppermute | solution.py:334
  70.7 1.9 collective-permute-done.4.refs_4_
  72.7 2.1 %collective-permute-done.6.refs_6_ = f32[2,64,128]{2,1,0:T(8,128)S(1)} collective-permute-done((f32[2,64,128]{2,1,0:T(8,128)}, f32[2,64,128]{2,1,0:T(8,128)S(1)}, u32[]{:S(2)}, u32[]{:S(2)}) %collective-permute-start.6) | collective-permute-done | bytes 65568 | tf_op jit(solution)/shard_map/ppermute | solution.py:334
  74.8 1.4 copy-done.4
  76.2 1.4 copy-done.20
  77.6 5.5 %basin_s1.1 = (f32[6,16,64,128]{3,2,1,0:T(8,128)S(1)}, f32[48,2,128]{2,1,0:T(2,128)S(1)}, f32[48,2,128]{2,1,0:T(2,128)S(1)}, f32[2,64,128]{2,1,0:T(8,128)S(1)}) custom-call(s32[4]{0:T(128)S(1)} %add_convert_fusion.refs_0_, f32[3,16,64,128]{3,2,1,0:T(8,128)S(1)} %copy-done.20, f32[6,16,64,128]{3,2,1,0:T(8,128)S(1)} %copy-done.2, ...), custom_call_target="tpu_custom_call" | custom-call | flops 23592960 | bytes 6291456 | tf_op jit(solution)/shard_map/basin_s1/pallas_call | solution.py:368
  83.1 1.7 copy-done.12
  86.6 2.2 %copy-done.6 = f32[1,1,64,128,128]{4,3,2,1,0:T(8,128)S(1)} copy-done((f32[1,1,64,128,128]{4,3,2,1,0:T(8,128)S(1)}, f32[1,1,64,128,128]{4,3,2,1,0:T(8,128)}, u32[]{:S(2)}) %copy-start.6) | copy-done | bytes 4194328
  88.8 2.2 %copy-done.8 = f32[1,1,64,128,128]{4,3,2,1,0:T(8,128)S(1)} copy-done((f32[1,1,64,128,128]{4,3,2,1,0:T(8,128)S(1)}, f32[1,1,64,128,128]{4,3,2,1,0:T(8,128)}, u32[]{:S(2)}) %copy-start.8) | copy-done | bytes 4194328
  92.5 14.4 %force1.1 = (f32[3,64,128]{2,1,0:T(8,128)S(1)}, f32[64,8,128]{2,1,0:T(8,128)S(1)}) custom-call(s32[64]{0:T(128)S(1)} %get-tuple-element.71.refs_0_, s32[64]{0:T(128)S(1)} %get-tuple-element.70.refs_1_, s32[64,128]{1,0:T(8,128)S(1)} %get-tuple-element.74.refs_2_, s32[64,128]{1,0:T(8,128)S(1)} %copy-done.35, s32[64,128]{1,0:T(8,128)S(1)} %copy-done.33, ...), custom_call_target="tpu_custom_call" | custom-call | flops 1073741824 | bytes 8388608 | tf_op jit(solution)/shard_map/force1/pallas_call | solution.py:417
  107.0 3.5 %box_v1.1 = (f32[3,8,64,128]{3,2,1,0:T(8,128)S(1)}, f32[72,2,128]{2,1,0:T(2,128)S(1)}, f32[72,2,128]{2,1,0:T(2,128)S(1)}, f32[3,64,128]{2,1,0:T(8,128)S(1)}) custom-call(s32[4]{0:T(128)S(1)} %add_convert_fusion.refs_0_, f32[3,8,64,128]{3,2,1,0:T(8,128)S(1)} %copy-done.29, f32[6,8,64,128]{3,2,1,0:T(8,128)S(1)} %copy-done.11, ...), custom_call_target="tpu_custom_call" | custom-call | flops 11796480 | bytes 3145728 | tf_op jit(solution)/shard_map/box_v1/pallas_call | solution.py:353
  110.5 3.7 %collective-permute-start.11 = (f32[3,64,128]{2,1,0:T(8,128)S(1)}, f32[3,64,128]{2,1,0:T(8,128)S(1)}, u32[]{:S(2)}, u32[]{:S(2)}) collective-permute-start(f32[3,64,128]{2,1,0:T(8,128)S(1)} %get-tuple-element.55), channel_id=1, source_target_pairs={{0,7},{1,0},{2,1},{3,2},{4,3},{5,4},{6,5},{7,6},{8,15},{9,8},{10,9... | collective-permute-start | bytes 294920 | tf_op jit(solution)/shard_map/ppermute | solution.py:334
  114.2 3.9 %collective-permute-start.9 = (f32[72,2,128]{2,1,0:T(2,128)S(1)}, f32[72,2,128]{2,1,0:T(2,128)S(1)}, u32[]{:S(2)}, u32[]{:S(2)}) collective-permute-start(f32[72,2,128]{2,1,0:T(2,128)S(1)} %get-tuple-element.54), channel_id=1, source_target_pairs={{0,120},{8,0},{16,8},{24,16},{32,24},{40,32},{48,40},{56,48},{64,5... | collective-permute-start | bytes 221192 | tf_op jit(solution)/shard_map/ppermute | solution.py:334
  118.1 2.0 %collective-permute-done.8.refs_4_ = f32[72,2,128]{2,1,0:T(2,128)S(1)} collective-permute-done((f32[72,2,128]{2,1,0:T(2,128)S(1)}, f32[72,2,128]{2,1,0:T(2,128)S(1)}, u32[]{:S(2)}, u32[]{:S(2)}) %collective-permute-start.8) | collective-permute-done | bytes 73760 | tf_op jit(solution)/shard_map/ppermute | solution.py:334
  120.1 2.3 %collective-permute-done.10.refs_6_ = f32[3,64,128]{2,1,0:T(8,128)S(1)} collective-permute-done((f32[3,64,128]{2,1,0:T(8,128)S(1)}, f32[3,64,128]{2,1,0:T(8,128)S(1)}, u32[]{:S(2)}, u32[]{:S(2)}) %collective-permute-start.10) | collective-permute-done | bytes 98336 | tf_op jit(solution)/shard_map/ppermute | solution.py:334
  122.4 6.5 %basin_v2.1 = (f32[3,16,64,128]{3,2,1,0:T(8,128)}, f32[48,2,128]{2,1,0:T(2,128)S(1)}, f32[48,2,128]{2,1,0:T(2,128)S(1)}, f32[2,64,128]{2,1,0:T(8,128)S(1)}) custom-call(s32[4]{0:T(128)S(1)} %add_convert_fusion.refs_0_, f32[3,16,64,128]{3,2,1,0:T(8,128)S(1)} %copy-done.21, f32[6,16,64,128]{3,2,1,0:T(8,128)S(1)} %copy-done.13, ...), custom_call_target="tpu_custom_call" | custom-call | flops 23592960 | bytes 6291456 | tf_op jit(solution)/shard_map/basin_v2/pallas_call | solution.py:353
  132.7 4.8 %all-to-all-start.1 = ((f32[8,3,64,128]{3,2,1,0:T(8,128)}), f32[8,3,64,128]{3,2,1,0:T(8,128)}, u32[]{:S(2)}, u32[]{:S(2)}) async-start(f32[8,3,64,128]{3,2,1,0:T(8,128)} %broadcast_in_dim.15), calls=%async_computation.1 | async-start | bytes 1572864 | tf_op jit(solution)/shard_map/all_to_all | solution.py:389
  142.5 3.6 %box_s1.1 = (f32[6,8,64,128]{3,2,1,0:T(8,128)S(1)}, f32[24,2,128]{2,1,0:T(2,128)}, f32[24,2,128]{2,1,0:T(2,128)}, f32[1,64,128]{2,1,0:T(8,128)}) custom-call(s32[4]{0:T(128)S(1)} %add_convert_fusion.refs_0_, f32[3,8,64,128]{3,2,1,0:T(8,128)S(1)} %copy-done.25, f32[6,8,64,128]{3,2,1,0:T(8,128)S(1)} %copy-done.11, f32[3,8,64,128]{3,2,1,0:T(8,128)S(1)} %copy-done.17, ...), custom_call_target="tpu_custom_call" | custom-call | flops 11796480 | bytes 3145728 | tf_op jit(solution)/shard_map/box_s1/pallas_call | solution.py:368
  147.3 5.6 %collective-permute-start.15 = (f32[1,64,128]{2,1,0:T(8,128)}, f32[1,64,128]{2,1,0:T(8,128)S(1)}, u32[]{:S(2)}, u32[]{:S(2)}) collective-permute-start(f32[1,64,128]{2,1,0:T(8,128)} %get-tuple-element.61), channel_id=1, source_target_pairs={{0,7},{1,0},{2,1},{3,2},{4,3},{5,4},{6,5},{7,6},{8,15},{9,8},{10,9... | collective-permute-start | bytes 98312 | tf_op jit(solution)/shard_map/ppermute | solution.py:334
  152.9 3.9 %collective-permute-start.13 = (f32[24,2,128]{2,1,0:T(2,128)}, f32[24,2,128]{2,1,0:T(2,128)S(1)}, u32[]{:S(2)}, u32[]{:S(2)}) collective-permute-start(f32[24,2,128]{2,1,0:T(2,128)} %get-tuple-element.60), channel_id=1, source_target_pairs={{0,120},{8,0},{16,8},{24,16},{32,24},{40,32},{48,40},{56,48},{64,5... | collective-permute-start | bytes 73736 | tf_op jit(solution)/shard_map/ppermute | solution.py:334
  156.8 2.2 %copy-done.7 = f32[1,1,64,128,128]{4,3,2,1,0:T(8,128)S(1)} copy-done((f32[1,1,64,128,128]{4,3,2,1,0:T(8,128)S(1)}, f32[1,1,64,128,128]{4,3,2,1,0:T(8,128)}, u32[]{:S(2)}) %copy-start.7) | copy-done | bytes 4194328
  159.0 2.2 %copy-done.9 = f32[1,1,64,128,128]{4,3,2,1,0:T(8,128)S(1)} copy-done((f32[1,1,64,128,128]{4,3,2,1,0:T(8,128)S(1)}, f32[1,1,64,128,128]{4,3,2,1,0:T(8,128)}, u32[]{:S(2)}) %copy-start.9) | copy-done | bytes 4194328
  163.7 11.4 %force2.1.refs_8_ = f32[3,64,128]{2,1,0:T(8,128)S(1)} custom-call(s32[64]{0:T(128)S(1)} %get-tuple-element.71.refs_0_, s32[64]{0:T(128)S(1)} %get-tuple-element.70.refs_1_, s32[64,128]{1,0:T(8,128)S(1)} %get-tuple-element.74.refs_2_, s32[64,128]{1,0:T(8,128)S(1)} %copy-done.36, s32[64,128]{1,0:T(8,128)S(1)} %copy-done.34, ...), custom_call_target="tpu_custom_call" | custom-call | flops 1073741824 | bytes 8388608 | tf_op jit(solution)/shard_map/force2/pallas_call | solution.py:417
  175.2 3.8 %box_v2.1 = (f32[3,8,64,128]{3,2,1,0:T(8,128)}, f32[72,2,128]{2,1,0:T(2,128)S(1)}, f32[72,2,128]{2,1,0:T(2,128)S(1)}, f32[3,64,128]{2,1,0:T(8,128)S(1)}) custom-call(s32[4]{0:T(128)S(1)} %add_convert_fusion.refs_0_, f32[3,8,64,128]{3,2,1,0:T(8,128)S(1)} %copy-done.26, f32[6,8,64,128]{3,2,1,0:T(8,128)S(1)} %copy-done.23, f32[3,8,64,128]{3,2,1,0:T(8,128)S(1)} %copy-done.18, ...), custom_call_target="tpu_custom_call" | custom-call | flops 11796480 | bytes 3145728 | tf_op jit(solution)/shard_map/box_v2/pallas_call | solution.py:353
  178.9 5.3 %collective-permute-start.19 = (f32[3,64,128]{2,1,0:T(8,128)S(1)}, f32[3,64,128]{2,1,0:T(8,128)S(1)}, u32[]{:S(2)}, u32[]{:S(2)}) collective-permute-start(f32[3,64,128]{2,1,0:T(8,128)S(1)} %get-tuple-element.68), channel_id=1, source_target_pairs={{0,7},{1,0},{2,1},{3,2},{4,3},{5,4},{6,5},{7,6},{8,15},{9,8},{10,9... | collective-permute-start | bytes 294920 | tf_op jit(solution)/shard_map/ppermute | solution.py:334
  184.3 3.9 %collective-permute-start.17 = (f32[72,2,128]{2,1,0:T(2,128)S(1)}, f32[72,2,128]{2,1,0:T(2,128)S(1)}, u32[]{:S(2)}, u32[]{:S(2)}) collective-permute-start(f32[72,2,128]{2,1,0:T(2,128)S(1)} %get-tuple-element.67), channel_id=1, source_target_pairs={{0,120},{8,0},{16,8},{24,16},{32,24},{40,32},{48,40},{56,48},{64,5... | collective-permute-start | bytes 221192 | tf_op jit(solution)/shard_map/ppermute | solution.py:334
  188.1 2.0 %collective-permute-done.16.refs_4_ = f32[72,2,128]{2,1,0:T(2,128)S(1)} collective-permute-done((f32[72,2,128]{2,1,0:T(2,128)S(1)}, f32[72,2,128]{2,1,0:T(2,128)S(1)}, u32[]{:S(2)}, u32[]{:S(2)}) %collective-permute-start.16) | collective-permute-done | bytes 73760 | tf_op jit(solution)/shard_map/ppermute | solution.py:334
  190.2 2.3 %collective-permute-done.18.refs_6_ = f32[3,64,128]{2,1,0:T(8,128)S(1)} collective-permute-done((f32[3,64,128]{2,1,0:T(8,128)S(1)}, f32[3,64,128]{2,1,0:T(8,128)S(1)}, u32[]{:S(2)}, u32[]{:S(2)}) %collective-permute-start.18) | collective-permute-done | bytes 98336 | tf_op jit(solution)/shard_map/ppermute | solution.py:334
  192.5 6.0 %basin_s2.1 = f32[6,16,64,128]{3,2,1,0:T(8,128)} custom-call(s32[4]{0:T(128)S(1)} %add_convert_fusion.refs_0_, f32[3,16,64,128]{3,2,1,0:T(8,128)S(1)} %copy-done.27, f32[6,16,64,128]{3,2,1,0:T(8,128)S(1)} %copy-done.14, f32[3,16,64,128]{3,2,1,0:T(8,128)S(1)} %copy-done.5, f32[72,2,128]{2,1,0:T(2,128)S(1)} %collective-permute-done.16.refs_4_, ...), custom_call_target="tpu_custom_call" | custom-call | flops 23592960 | bytes 6291456 | tf_op jit(solution)/shard_map/basin_s2/pallas_call | solution.py:368
  198.5 3.5 %box_s2.1 = f32[6,8,64,128]{3,2,1,0:T(8,128)} custom-call(s32[4]{0:T(128)S(1)} %add_convert_fusion.refs_0_, f32[3,8,64,128]{3,2,1,0:T(8,128)S(1)} %copy-done.30, f32[6,8,64,128]{3,2,1,0:T(8,128)S(1)} %copy-done.23, f32[3,8,64,128]{3,2,1,0:T(8,128)S(1)} %copy-done.18, f32[72,2,128]{2,1,0:T(2,128)S(1)} %collective-permute-done.16.refs_4_, ...), custom_call_target="tpu_custom_call" | custom-call | flops 11796480 | bytes 3145728 | tf_op jit(solution)/shard_map/box_s2/pallas_call | solution.py:368
  (143 shorter events, 21.2 us)
Async XLA Ops:
  0.6 41.4 %copy-start = (s32[1,8,8192]{2,1,0:T(8,128)S(1)}, s32[1,8,8192]{2,1,0:T(8,128)}, u32[]{:S(2)}) copy-start(s32[1,8,8192]{2,1,0:T(8,128)} %param.19) | copy-start | bytes 786436
  5.6 18.9 %copy-start.2 = (f32[6,16,64,128]{3,2,1,0:T(8,128)S(1)}, f32[6,16,64,128]{3,2,1,0:T(8,128)}, u32[]{:S(2)}) copy-start(f32[6,16,64,128]{3,2,1,0:T(8,128)} %refs_2_.5) | copy-start | bytes 9437188
  10.4 12.9 %collective-permute-start.3 = (f32[3,64,128]{2,1,0:T(8,128)}, f32[3,64,128]{2,1,0:T(8,128)S(1)}, u32[]{:S(2)}, u32[]{:S(2)}) collective-permute-start(f32[3,64,128]{2,1,0:T(8,128)} %get-tuple-element.40), channel_id=1, source_target_pairs={{0,7},{1,0},{2,1},{3,2},{4,3},{5,4},{6,5},{7,6},{8,15},{9,8},{10,9... | collective-permute-start | bytes 294920 | tf_op jit(solution)/shard_map/ppermute | solution.py:334
  15.9 8.5 %collective-permute-start.2 = (f32[3,64,128]{2,1,0:T(8,128)}, f32[3,64,128]{2,1,0:T(8,128)}, u32[]{:S(2)}, u32[]{:S(2)}) collective-permute-start(f32[3,64,128]{2,1,0:T(8,128)} %get-tuple-element.40), channel_id=1, source_target_pairs={{0,1},{1,2},{2,3},{3,4},{4,5},{5,6},{6,7},{7,0},{8,9},{9,10},{10,1... | collective-permute-start | bytes 294920 | tf_op jit(solution)/shard_map/ppermute | solution.py:334
  15.9 7.3 %collective-permute-start = (f32[72,2,128]{2,1,0:T(2,128)}, f32[72,2,128]{2,1,0:T(2,128)}, u32[]{:S(2)}, u32[]{:S(2)}) collective-permute-start(f32[72,2,128]{2,1,0:T(2,128)} %get-tuple-element.38), channel_id=1, source_target_pairs={{0,8},{8,16},{16,24},{24,32},{32,40},{40,48},{48,56},{56,64},{64,7... | collective-permute-start | bytes 221192 | tf_op jit(solution)/shard_map/ppermute | solution.py:334
  15.9 7.3 %collective-permute-start.1 = (f32[72,2,128]{2,1,0:T(2,128)}, f32[72,2,128]{2,1,0:T(2,128)}, u32[]{:S(2)}, u32[]{:S(2)}) collective-permute-start(f32[72,2,128]{2,1,0:T(2,128)} %get-tuple-element.39), channel_id=1, source_target_pairs={{0,120},{8,0},{16,8},{24,16},{32,24},{40,32},{48,40},{56,48},{64,5... | collective-permute-start | bytes 221192 | tf_op jit(solution)/shard_map/ppermute | solution.py:334
  36.3 50.3 %all-to-all-start = ((f32[8,6,64,128]{3,2,1,0:T(8,128)}), f32[8,6,64,128]{3,2,1,0:T(8,128)}, u32[]{:S(2)}, u32[]{:S(2)}) async-start(f32[8,6,64,128]{3,2,1,0:T(8,128)} %broadcast_in_dim.6), calls=%async_computation | async-start | bytes 3145728 | tf_op jit(solution)/shard_map/all_to_all | solution.py:389
  61.1 11.6 %collective-permute-start.7 = (f32[2,64,128]{2,1,0:T(8,128)}, f32[2,64,128]{2,1,0:T(8,128)S(1)}, u32[]{:S(2)}, u32[]{:S(2)}) collective-permute-start(f32[2,64,128]{2,1,0:T(8,128)} %copy-done.57), channel_id=1, source_target_pairs={{0,7},{1,0},{2,1},{3,2},{4,3},{5,4},{6,5},{7,6},{8,15},{9,8},{10,9... | collective-permute-start | bytes 196616 | tf_op jit(solution)/shard_map/ppermute | solution.py:334
  66.7 8.1 %collective-permute-start.6 = (f32[2,64,128]{2,1,0:T(8,128)}, f32[2,64,128]{2,1,0:T(8,128)S(1)}, u32[]{:S(2)}, u32[]{:S(2)}) collective-permute-start(f32[2,64,128]{2,1,0:T(8,128)} %copy-done.57), channel_id=1, source_target_pairs={{0,1},{1,2},{2,3},{3,4},{4,5},{5,6},{6,7},{7,0},{8,9},{9,10},{10,1... | collective-permute-start | bytes 196616 | tf_op jit(solution)/shard_map/ppermute | solution.py:334
  66.7 6.0 %collective-permute-start.4 = (f32[48,2,128]{2,1,0:T(2,128)}, f32[48,2,128]{2,1,0:T(2,128)S(1)}, u32[]{:S(2)}, u32[]{:S(2)}) collective-permute-start(f32[48,2,128]{2,1,0:T(2,128)} %copy-done.59), channel_id=1, source_target_pairs={{0,8},{8,16},{16,24},{24,32},{32,40},{40,48},{48,56},{56,64},{64,7... | collective-permute-start | bytes 147464 | tf_op jit(solution)/shard_map/ppermute | solution.py:334
  66.7 6.0 %collective-permute-start.5 = (f32[48,2,128]{2,1,0:T(2,128)}, f32[48,2,128]{2,1,0:T(2,128)S(1)}, u32[]{:S(2)}, u32[]{:S(2)}) collective-permute-start(f32[48,2,128]{2,1,0:T(2,128)} %copy-done.58), channel_id=1, source_target_pairs={{0,120},{8,0},{16,8},{24,16},{32,24},{40,32},{48,40},{56,48},{64,5... | collective-permute-start | bytes 147464 | tf_op jit(solution)/shard_map/ppermute | solution.py:334
  86.6 2.2 %copy-start.6 = (f32[1,1,64,128,128]{4,3,2,1,0:T(8,128)S(1)}, f32[1,1,64,128,128]{4,3,2,1,0:T(8,128)}, u32[]{:S(2)}) copy-start(f32[1,1,64,128,128]{4,3,2,1,0:T(8,128)} %param.20) | copy-start | bytes 12582916
  92.5 14.4 %copy-start.11 = (f32[6,8,64,128]{3,2,1,0:T(8,128)S(1)}, f32[6,8,64,128]{3,2,1,0:T(8,128)}, u32[]{:S(2)}) copy-start(f32[6,8,64,128]{3,2,1,0:T(8,128)} %refs_2_.7) | copy-start | bytes 4718596
  92.5 14.4 %copy-start.16 = (f32[3,8,64,128]{3,2,1,0:T(8,128)S(1)}, f32[3,8,64,128]{3,2,1,0:T(8,128)}, u32[]{:S(2)}) copy-start(f32[3,8,64,128]{3,2,1,0:T(8,128)} %copy-done.15) | copy-start | bytes 2359300
  92.5 14.4 %copy-start.29 = (f32[3,8,64,128]{3,2,1,0:T(8,128)S(1)}, f32[3,8,64,128]{3,2,1,0:T(8,128)}, u32[]{:S(2)}) copy-start(f32[3,8,64,128]{3,2,1,0:T(8,128)} %refs_1_.3) | copy-start | bytes 2359300
  92.5 14.4 %copy-start.45 = (f32[2,64,128]{2,1,0:T(8,128)S(1)}, f32[2,64,128]{2,1,0:T(8,128)}, u32[]{:S(2)}) copy-start(f32[2,64,128]{2,1,0:T(8,128)} %copy-done.44) | copy-start | bytes 196612
  92.5 14.5 %copy-start.49 = (f32[48,2,128]{2,1,0:T(2,128)S(1)}, f32[48,2,128]{2,1,0:T(2,128)}, u32[]{:S(2)}) copy-start(f32[48,2,128]{2,1,0:T(2,128)} %copy-done.48) | copy-start | bytes 147460
  92.5 14.5 %copy-start.51 = (f32[48,2,128]{2,1,0:T(2,128)S(1)}, f32[48,2,128]{2,1,0:T(2,128)}, u32[]{:S(2)}) copy-start(f32[48,2,128]{2,1,0:T(2,128)} %copy-done.50) | copy-start | bytes 147460
  92.5 29.9 %copy-start.13 = (f32[6,16,64,128]{3,2,1,0:T(8,128)S(1)}, f32[6,16,64,128]{3,2,1,0:T(8,128)}, u32[]{:S(2)}) copy-start(f32[6,16,64,128]{3,2,1,0:T(8,128)} %copy-done.12) | copy-start | bytes 9437188
  106.9 3.6 %copy-start.42 = (f32[64,8,128]{2,1,0:T(8,128)}, f32[64,8,128]{2,1,0:T(8,128)S(1)}, u32[]{:S(2)}) copy-start(f32[64,8,128]{2,1,0:T(8,128)S(1)} %get-tuple-element.62.refs_8_) | copy-start | bytes 786436
  107.0 15.5 %copy-start.5 = (f32[3,16,64,128]{3,2,1,0:T(8,128)S(1)}, f32[3,16,64,128]{3,2,1,0:T(8,128)}, u32[]{:S(2)}) copy-start(f32[3,16,64,128]{3,2,1,0:T(8,128)} %refs_3_.7) | copy-start | bytes 4718596
  107.0 15.5 %copy-start.21 = (f32[3,16,64,128]{3,2,1,0:T(8,128)S(1)}, f32[3,16,64,128]{3,2,1,0:T(8,128)}, u32[]{:S(2)}) copy-start(f32[3,16,64,128]{3,2,1,0:T(8,128)} %copy-done.19) | copy-start | bytes 4718596
  110.5 18.4 %copy-start.24 = (f32[3,8,64,128]{3,2,1,0:T(8,128)}, f32[3,8,64,128]{3,2,1,0:T(8,128)S(1)}, u32[]{:S(2)}) copy-start(f32[3,8,64,128]{3,2,1,0:T(8,128)S(1)} %get-tuple-element.57.refs_1_) | copy-start | bytes 2359300
  110.5 9.6 %collective-permute-start.11 = (f32[3,64,128]{2,1,0:T(8,128)S(1)}, f32[3,64,128]{2,1,0:T(8,128)S(1)}, u32[]{:S(2)}, u32[]{:S(2)}) collective-permute-start(f32[3,64,128]{2,1,0:T(8,128)S(1)} %get-tuple-element.55), channel_id=1, source_target_pairs={{0,7},{1,0},{2,1},{3,2},{4,3},{5,4},{6,5},{7,6},{8,15},{9,8},{10,9... | collective-permute-start | bytes 294920 | tf_op jit(solution)/shard_map/ppermute | solution.py:334
  114.2 8.2 %collective-permute-start.10 = (f32[3,64,128]{2,1,0:T(8,128)S(1)}, f32[3,64,128]{2,1,0:T(8,128)S(1)}, u32[]{:S(2)}, u32[]{:S(2)}) collective-permute-start(f32[3,64,128]{2,1,0:T(8,128)S(1)} %get-tuple-element.55), channel_id=1, source_target_pairs={{0,1},{1,2},{2,3},{3,4},{4,5},{5,6},{6,7},{7,0},{8,9},{9,10},{10,1... | collective-permute-start | bytes 294920 | tf_op jit(solution)/shard_map/ppermute | solution.py:334
  114.2 5.9 %collective-permute-start.8 = (f32[72,2,128]{2,1,0:T(2,128)S(1)}, f32[72,2,128]{2,1,0:T(2,128)S(1)}, u32[]{:S(2)}, u32[]{:S(2)}) collective-permute-start(f32[72,2,128]{2,1,0:T(2,128)S(1)} %get-tuple-element.53), channel_id=1, source_target_pairs={{0,8},{8,16},{16,24},{24,32},{32,40},{40,48},{48,56},{56,64},{64,7... | collective-permute-start | bytes 221192 | tf_op jit(solution)/shard_map/ppermute | solution.py:334
  114.2 5.9 %collective-permute-start.9 = (f32[72,2,128]{2,1,0:T(2,128)S(1)}, f32[72,2,128]{2,1,0:T(2,128)S(1)}, u32[]{:S(2)}, u32[]{:S(2)}) collective-permute-start(f32[72,2,128]{2,1,0:T(2,128)S(1)} %get-tuple-element.54), channel_id=1, source_target_pairs={{0,120},{8,0},{16,8},{24,16},{32,24},{40,32},{48,40},{56,48},{64,5... | collective-permute-start | bytes 221192 | tf_op jit(solution)/shard_map/ppermute | solution.py:334
  120.1 8.9 %copy-start.37 = (f32[72,2,128]{2,1,0:T(2,128)}, f32[72,2,128]{2,1,0:T(2,128)S(1)}, u32[]{:S(2)}) copy-start(f32[72,2,128]{2,1,0:T(2,128)S(1)} %collective-permute-done.8.refs_4_) | copy-start | bytes 221188
  120.1 8.9 %copy-start.39 = (f32[72,2,128]{2,1,0:T(2,128)}, f32[72,2,128]{2,1,0:T(2,128)S(1)}, u32[]{:S(2)}) copy-start(f32[72,2,128]{2,1,0:T(2,128)S(1)} %collective-permute-done.9.refs_5_) | copy-start | bytes 221188
  122.4 6.5 %copy-start.31 = (f32[3,64,128]{2,1,0:T(8,128)}, f32[3,64,128]{2,1,0:T(8,128)S(1)}, u32[]{:S(2)}) copy-start(f32[3,64,128]{2,1,0:T(8,128)S(1)} %collective-permute-done.10.refs_6_) | copy-start | bytes 294916
  132.7 24.0 %all-to-all-start.1 = ((f32[8,3,64,128]{3,2,1,0:T(8,128)}), f32[8,3,64,128]{3,2,1,0:T(8,128)}, u32[]{:S(2)}, u32[]{:S(2)}) async-start(f32[8,3,64,128]{3,2,1,0:T(8,128)} %broadcast_in_dim.15), calls=%async_computation.1 | async-start | bytes 1572864 | tf_op jit(solution)/shard_map/all_to_all | solution.py:389
  147.3 27.8 %collective-permute-start.15 = (f32[1,64,128]{2,1,0:T(8,128)}, f32[1,64,128]{2,1,0:T(8,128)S(1)}, u32[]{:S(2)}, u32[]{:S(2)}) collective-permute-start(f32[1,64,128]{2,1,0:T(8,128)} %get-tuple-element.61), channel_id=1, source_target_pairs={{0,7},{1,0},{2,1},{3,2},{4,3},{5,4},{6,5},{7,6},{8,15},{9,8},{10,9... | collective-permute-start | bytes 98312 | tf_op jit(solution)/shard_map/ppermute | solution.py:334
  152.9 22.2 %collective-permute-start.14 = (f32[1,64,128]{2,1,0:T(8,128)}, f32[1,64,128]{2,1,0:T(8,128)S(1)}, u32[]{:S(2)}, u32[]{:S(2)}) collective-permute-start(f32[1,64,128]{2,1,0:T(8,128)} %get-tuple-element.61), channel_id=1, source_target_pairs={{0,1},{1,2},{2,3},{3,4},{4,5},{5,6},{6,7},{7,0},{8,9},{9,10},{10,1... | collective-permute-start | bytes 98312 | tf_op jit(solution)/shard_map/ppermute | solution.py:334
  152.9 22.1 %collective-permute-start.12 = (f32[24,2,128]{2,1,0:T(2,128)}, f32[24,2,128]{2,1,0:T(2,128)S(1)}, u32[]{:S(2)}, u32[]{:S(2)}) collective-permute-start(f32[24,2,128]{2,1,0:T(2,128)} %get-tuple-element.59), channel_id=1, source_target_pairs={{0,8},{8,16},{16,24},{24,32},{32,40},{40,48},{48,56},{56,64},{64,7... | collective-permute-start | bytes 73736 | tf_op jit(solution)/shard_map/ppermute | solution.py:334
  152.9 22.2 %collective-permute-start.13 = (f32[24,2,128]{2,1,0:T(2,128)}, f32[24,2,128]{2,1,0:T(2,128)S(1)}, u32[]{:S(2)}, u32[]{:S(2)}) collective-permute-start(f32[24,2,128]{2,1,0:T(2,128)} %get-tuple-element.60), channel_id=1, source_target_pairs={{0,120},{8,0},{16,8},{24,16},{32,24},{40,32},{48,40},{56,48},{64,5... | collective-permute-start | bytes 73736 | tf_op jit(solution)/shard_map/ppermute | solution.py:334
  163.6 11.5 %copy-start.18 = (f32[3,8,64,128]{3,2,1,0:T(8,128)S(1)}, f32[3,8,64,128]{3,2,1,0:T(8,128)}, u32[]{:S(2)}) copy-start(f32[3,8,64,128]{3,2,1,0:T(8,128)} %copy-done.15) | copy-start | bytes 2359300
  163.6 11.5 %copy-start.23 = (f32[6,8,64,128]{3,2,1,0:T(8,128)S(1)}, f32[6,8,64,128]{3,2,1,0:T(8,128)}, u32[]{:S(2)}) copy-start(f32[6,8,64,128]{3,2,1,0:T(8,128)} %copy-done.22) | copy-start | bytes 4718596
  163.6 11.5 %copy-start.26 = (f32[3,8,64,128]{3,2,1,0:T(8,128)S(1)}, f32[3,8,64,128]{3,2,1,0:T(8,128)}, u32[]{:S(2)}) copy-start(f32[3,8,64,128]{3,2,1,0:T(8,128)} %copy-done.24) | copy-start | bytes 2359300
  163.6 11.5 %copy-start.47 = (f32[2,64,128]{2,1,0:T(8,128)S(1)}, f32[2,64,128]{2,1,0:T(8,128)}, u32[]{:S(2)}) copy-start(f32[2,64,128]{2,1,0:T(8,128)} %copy-done.46) | copy-start | bytes 196612
  163.6 11.5 %copy-start.53 = (f32[48,2,128]{2,1,0:T(2,128)S(1)}, f32[48,2,128]{2,1,0:T(2,128)}, u32[]{:S(2)}) copy-start(f32[48,2,128]{2,1,0:T(2,128)} %copy-done.52) | copy-start | bytes 147460
  163.6 11.5 %copy-start.55 = (f32[48,2,128]{2,1,0:T(2,128)S(1)}, f32[48,2,128]{2,1,0:T(2,128)}, u32[]{:S(2)}) copy-start(f32[48,2,128]{2,1,0:T(2,128)} %copy-done.54) | copy-start | bytes 147460
  163.6 28.9 %copy-start.27 = (f32[3,16,64,128]{3,2,1,0:T(8,128)S(1)}, f32[3,16,64,128]{3,2,1,0:T(8,128)}, u32[]{:S(2)}) copy-start(f32[3,16,64,128]{3,2,1,0:T(8,128)} %get-tuple-element.34.refs_1_) | copy-start | bytes 4718596
  175.2 17.4 %copy-start.14 = (f32[6,16,64,128]{3,2,1,0:T(8,128)S(1)}, f32[6,16,64,128]{3,2,1,0:T(8,128)}, u32[]{:S(2)}) copy-start(f32[6,16,64,128]{3,2,1,0:T(8,128)} %copy-done.12) | copy-start | bytes 9437188
  178.9 11.2 %collective-permute-start.19 = (f32[3,64,128]{2,1,0:T(8,128)S(1)}, f32[3,64,128]{2,1,0:T(8,128)S(1)}, u32[]{:S(2)}, u32[]{:S(2)}) collective-permute-start(f32[3,64,128]{2,1,0:T(8,128)S(1)} %get-tuple-element.68), channel_id=1, source_target_pairs={{0,7},{1,0},{2,1},{3,2},{4,3},{5,4},{6,5},{7,6},{8,15},{9,8},{10,9... | collective-permute-start | bytes 294920 | tf_op jit(solution)/shard_map/ppermute | solution.py:334
  184.3 8.2 %collective-permute-start.18 = (f32[3,64,128]{2,1,0:T(8,128)S(1)}, f32[3,64,128]{2,1,0:T(8,128)S(1)}, u32[]{:S(2)}, u32[]{:S(2)}) collective-permute-start(f32[3,64,128]{2,1,0:T(8,128)S(1)} %get-tuple-element.68), channel_id=1, source_target_pairs={{0,1},{1,2},{2,3},{3,4},{4,5},{5,6},{6,7},{7,0},{8,9},{9,10},{10,1... | collective-permute-start | bytes 294920 | tf_op jit(solution)/shard_map/ppermute | solution.py:334
  184.3 5.9 %collective-permute-start.16 = (f32[72,2,128]{2,1,0:T(2,128)S(1)}, f32[72,2,128]{2,1,0:T(2,128)S(1)}, u32[]{:S(2)}, u32[]{:S(2)}) collective-permute-start(f32[72,2,128]{2,1,0:T(2,128)S(1)} %get-tuple-element.66), channel_id=1, source_target_pairs={{0,8},{8,16},{16,24},{24,32},{32,40},{40,48},{48,56},{56,64},{64,7... | collective-permute-start | bytes 221192 | tf_op jit(solution)/shard_map/ppermute | solution.py:334
  184.3 14.3 %copy-start.30 = (f32[3,8,64,128]{3,2,1,0:T(8,128)S(1)}, f32[3,8,64,128]{3,2,1,0:T(8,128)}, u32[]{:S(2)}) copy-start(f32[3,8,64,128]{3,2,1,0:T(8,128)} %get-tuple-element.36.refs_1_) | copy-start | bytes 2359300
  184.3 5.9 %collective-permute-start.17 = (f32[72,2,128]{2,1,0:T(2,128)S(1)}, f32[72,2,128]{2,1,0:T(2,128)S(1)}, u32[]{:S(2)}, u32[]{:S(2)}) collective-permute-start(f32[72,2,128]{2,1,0:T(2,128)S(1)} %get-tuple-element.67), channel_id=1, source_target_pairs={{0,120},{8,0},{16,8},{24,16},{32,24},{40,32},{48,40},{56,48},{64,5... | collective-permute-start | bytes 221192 | tf_op jit(solution)/shard_map/ppermute | solution.py:334
  (34 other events, 38.8 us)

commit v2 on v1

--- a/solution.py
+++ b/solution.py
@@ -21,7 +21,8 @@
 
 VM = pl.BlockSpec(memory_space=pltpu.VMEM)
 SM = pl.BlockSpec(memory_space=pltpu.SMEM)
-PARAMS = pltpu.CompilerParams(vmem_limit_bytes=20 * 2**20)
+HB = pl.BlockSpec(memory_space=pltpu.HBM)
+PARAMS = pltpu.CompilerParams(vmem_limit_bytes=56 * 2**20)
 F32 = jnp.float32
 BF16 = jnp.bfloat16
 XS = (0, 1, 2)
@@ -64,7 +65,7 @@
         qm_ref[j] = jnp.where(part < 2, left, right)
 
 
-def fill_pad(flags_ref, src_ref, comps, xb_ref, xa_ref, k0, pad_ref, layers):
+def fill_pad(flags_ref, src_ref, comps, xb_ref, xa_ref, k0, pad_ref, layers, group):
     def body(z, _):
         for i, c in enumerate(comps):
             k = k0 + i * layers + z
@@ -73,7 +74,7 @@
             pad_ref[i, z, 8 + CX : 10 + CX] = jnp.where(flags_ref[1] > 0, xa_ref[k], 0.0)
         return 0
 
-    lax.fori_loop(0, layers, body, 0)
+    lax.fori_loop(*group, body, 0)
 
 
 def dx(pad_ref, i, z, forward):
@@ -85,13 +86,37 @@
     return NEAR * (at(0) - at(-1)) - FAR * (at(1) - at(-2))
 
 
-def dy(value, halo, forward):
-    lane = lanes()
-    before = pltpu.roll(jnp.where(lane >= CY - 1, halo, value), 1, 1)
-    after = pltpu.roll(jnp.where(lane < 1, halo, value), CY - 1, 1)
-    if forward:
-        return NEAR * (after - value) - FAR * (pltpu.roll(jnp.where(lane < 2, halo, value), CY - 2, 1) - before)
-    return NEAR * (value - before) - FAR * (after - pltpu.roll(jnp.where(lane >= CY - 2, halo, value), 2, 1))
+def fill_weights(w_ref):
+    at = lax.broadcasted_iota(jnp.int32, (CY, CY), 0)
+    to = lax.broadcasted_iota(jnp.int32, (CY, CY), 1)
+    beyond = jnp.where(at >= CY - 2, at - CY, jnp.where(at < 2, at + CY, -CY))
+    for forward in range(2):
+        for part, source in enumerate((at, beyond)):
+            offset = source - to - forward
+            weight = jnp.where(offset == 0, 27.0, jnp.where(offset == -1, -27.0, 0.0))
+            weight = jnp.where(offset == 1, -1.0, jnp.where(offset == -2, 1.0, weight)).astype(BF16)
+            for copy in range(2):
+                low = (2 * part + copy) * CY
+                w_ref[forward, low : low + CY] = weight
+
+
+def pieces(value):
+    high = value.astype(BF16)
+    return high, (value - high.astype(F32)).astype(BF16)
+
+
+def fill_dy(group, src_ref, comps, forward, qm_ref, k0, layers, w_ref, t_ref, y_ref):
+    a, b = group
+    for i, c in enumerate(comps):
+        j, m = slot(k0, layers, i)
+        for z in range(a, b):
+            low = (z - a) * CX
+            terms = (*pieces(src_ref[c, z]), *pieces(y_halo(qm_ref, j, m + z)))
+            for n, term in enumerate(terms):
+                t_ref[i, low : low + CX, n * CY : (n + 1) * CY] = term
+        result = jnp.dot(t_ref[i], w_ref[forward[i]], preferred_element_type=F32) * (1.0 / 24.0)
+        for z in range(a, b):
+            y_ref[i, z] = result[(z - a) * CX : (z - a + 1) * CX]
 
 
 def dz(src_ref, c, z, layers, forward, edge):
@@ -105,32 +130,52 @@
     return NEAR * (at(0) - at(-1)) - FAR * (at(1) - at(-2))
 
 
-def over_layers(layers, body):
-    for z in (0, 1):
+def over_layers(layers, group, body):
+    low, high = max(group[0], 2), min(group[1], layers - 2)
+    for z in range(group[0], low):
         body(z, True)
 
     def inner(z, _):
         body(z, False)
         return 0
 
-    lax.fori_loop(2, layers - 2, inner, 0)
-    for z in (layers - 2, layers - 1):
+    lax.fori_loop(low, high, inner, 0)
+    for z in range(high, group[1]):
         body(z, True)
 
 
-def pack_kernel(zm_ref, sb_ref, sx_ref, ids_ref, xlo_ref, xhi_ref, q_ref, med_ref):
+def groups_of(layers):
+    return [(z, z + 4) for z in range(0, layers, 4)]
+
+
+def streams(pairs, sem_ref, layers):
+    return [
+        [
+            pltpu.make_async_copy(src.at[:, a:b], dst.at[:, a:b], sem_ref.at[p, n])
+            for p, (src, dst) in enumerate(pairs)
+        ]
+        for n, (a, b) in enumerate(groups_of(layers))
+    ]
+
+
+def start_all(copies):
+    for group in copies:
+        for copy in group:
+            copy.start()
+
+
+def wait_group(copies, n):
+    if n < len(copies):
+        for copy in copies[n]:
+            copy.wait()
+
+
+def pack_kernel(zm_ref, sb_ref, sx_ref, ids_ref, xlo_ref, xhi_ref, q_ref, med_ref, b_ref, x_ref, b_sem, x_sem):
+    copies_b = streams(((sb_ref.at[0:5], b_ref),), b_sem, NZ)
+    copies_x = streams(((sx_ref.at[0:5], x_ref),), x_sem, BZ)
+    start_all(copies_b)
+    start_all(copies_x)
     q_ref[...] = jnp.zeros(q_ref.shape, F32)
-    for ref, layers, k0 in ((sb_ref, NZ, 0), (sx_ref, BZ, 3 * NZ)):
-
-        def body(z, _, ref=ref, layers=layers, k0=k0):
-            for i, c in enumerate(XS):
-                put_x(xlo_ref, xhi_ref, k0 + i * layers + z, ref[c, z])
-            for i, c in enumerate(YS):
-                j, m = slot(k0, layers, i)
-                put_y(q_ref, j, m + z, ref[c, z])
-            return 0
-
-        lax.fori_loop(0, layers, body, 0)
 
     def media(z, _):
         ids = ids_ref[z]
@@ -142,6 +187,19 @@
         return 0
 
     lax.fori_loop(0, BZ, media, 0)
+    for ref, copies, layers, k0 in ((b_ref, copies_b, NZ, 0), (x_ref, copies_x, BZ, 3 * NZ)):
+
+        def body(z, _, ref=ref, layers=layers, k0=k0):
+            for i, c in enumerate(XS):
+                put_x(xlo_ref, xhi_ref, k0 + i * layers + z, ref[c, z])
+            for i, c in enumerate(YS):
+                j, m = slot(k0, layers, i)
+                put_y(q_ref, j, m + z, ref[c, z])
+            return 0
+
+        for n, group in enumerate(groups_of(layers)):
+            wait_group(copies, n)
+            lax.fori_loop(*group, body, 0)
 
 
 def start_edges(carried, xlo_ref, xhi_ref, q_ref):
@@ -155,27 +213,49 @@
     return done
 
 
-def vel_kernel(layers, k0, forced, carry, *refs):
+def sweep(layers, copies, results, body, prepare, finish=True):
+    wait_group(copies, 0)
+    for n, group in enumerate(groups_of(layers)):
+        wait_group(copies, n + 1)
+        prepare(group)
+        over_layers(layers, group, body)
+        for result in results[n]:
+            result.start()
+    for n in range(len(results) if finish else 0):
+        wait_group(results, n)
+
+
+def vel_kernel(layers, k0, forced, carry, *refs, before=None, sent=0):
     flags_ref, v_ref, s_ref, med_ref, xb_ref, xa_ref, ql_ref, qr_ref = refs[:8]
     refs = refs[8:]
     if forced:
         force_ref, refs = refs[0], refs[1:]
     carried, refs = (refs[:3], refs[3:]) if carry else ((), refs)
-    out_ref, xlo_ref, xhi_ref, q_ref, pad_ref, qm_ref = refs
-    fill_pad(flags_ref, s_ref, XS, xb_ref, xa_ref, k0, pad_ref, layers)
+    hbm_v, hbm_s, hbm_med = v_ref, s_ref, med_ref
+    hbm_out, xlo_ref, xhi_ref, q_ref = refs[:4]
+    refs = refs[4:]
+    if sent:
+        hbm_sent, refs = refs[0], refs[1:]
+    pad_ref, qm_ref, w_ref, t_ref, y_ref, v_ref, s_ref, med_ref, out_ref, in_sem, out_sem, *sent_sem = refs
+    copies = streams(((hbm_s, s_ref), (hbm_v, v_ref), (hbm_med.at[2:3], med_ref)), in_sem, layers)
+    results = streams(((out_ref, hbm_out),), out_sem, layers)
+    for t in range(hbm_sent.shape[0] if sent else 0):
+        results[ZR // 4].append(pltpu.make_async_copy(out_ref.at[:, ZR], hbm_sent.at[t, sent - 3 : sent], sent_sem[0].at[1, t]))
+        if sent == 6:
+            results[ZR // 4].append(pltpu.make_async_copy(v_ref.at[:, ZR], hbm_sent.at[t, 0:3], sent_sem[0].at[0, t]))
+    start_all(copies)
+    fill_weights(w_ref)
     merge_q(flags_ref, ql_ref, qr_ref, qm_ref)
     o0 = start_edges(carried, xlo_ref, xhi_ref, q_ref)
+    if before:
+        before()
 
     def body(z, edge):
-        def ydiff(i, forward):
-            j, m = slot(k0, layers, i)
-            return dy(s_ref[YS[i], z], y_halo(qm_ref, j, m + z), forward)
-
-        scale = DT * med_ref[2, z]
+        scale = DT * med_ref[0, z]
         sums = (
-            dx(pad_ref, 0, z, True) + ydiff(0, False) + dz(s_ref, 1, z, layers, False, edge),
-            dx(pad_ref, 2, z, False) + ydiff(2, True) + dz(s_ref, 3, z, layers, False, edge),
-            dx(pad_ref, 1, z, False) + ydiff(1, False) + dz(s_ref, 5, z, layers, True, edge),
+            dx(pad_ref, 0, z, True) + y_ref[0, z] + dz(s_ref, 1, z, layers, False, edge),
+            dx(pad_ref, 2, z, False) + y_ref[2, z] + dz(s_ref, 3, z, layers, False, edge),
+            dx(pad_ref, 1, z, False) + y_ref[1, z] + dz(s_ref, 5, z, layers, True, edge),
         )
         for c in VS:
             new = v_ref[c, z] + scale * sums[c]
@@ -186,36 +266,38 @@
             j, m = slot(o0, layers, c)
             put_y(q_ref, j, m + z, new)
 
-    over_layers(layers, body)
-
-
-def stress_kernel(layers, k0, edges, *refs):
-    flags_ref, v_ref, s_ref, med_ref, xb_ref, xa_ref, ql_ref, qr_ref, out_ref = refs[:9]
+    def prepare(group):
+        fill_pad(flags_ref, s_ref, XS, xb_ref, xa_ref, k0, pad_ref, layers, group)
+        fill_dy(group, s_ref, YS, (0, 0, 1), qm_ref, k0, layers, w_ref, t_ref, y_ref)
+
+    sweep(layers, copies, results, body, prepare)
+
+
+def stress_parts(layers, k0, edges, *refs):
+    flags_ref, hbm_v, hbm_s, hbm_med, xb_ref, xa_ref, ql_ref, qr_ref, hbm_out = refs[:9]
     refs = refs[9:]
     if edges:
         xlo_ref, xhi_ref, q_ref = refs[:3]
         refs = refs[3:]
         q_ref[...] = jnp.zeros(q_ref.shape, F32)
-    pad_ref, qm_ref = refs
-    fill_pad(flags_ref, v_ref, VS, xb_ref, xa_ref, k0, pad_ref, layers)
+    pad_ref, qm_ref, w_ref, t_ref, y_ref, v_ref, s_ref, med_ref, out_ref, in_sem, out_sem = refs
+    copies = streams(((hbm_v, v_ref), (hbm_s, s_ref), (hbm_med.at[0:2], med_ref)), in_sem, layers)
+    results = streams(((out_ref, hbm_out),), out_sem, layers)
+    start_all(copies)
+    fill_weights(w_ref)
     merge_q(flags_ref, ql_ref, qr_ref, qm_ref)
 
     def body(z, edge):
-        def halo(c):
-            j, m = slot(k0, layers, c)
-            return y_halo(qm_ref, j, m + z)
-
         lam, mu = DT * med_ref[0, z], DT * med_ref[1, z]
         mod = lam + 2.0 * mu
-        hx, hy, hz = halo(0), halo(1), halo(2)
         ex = dx(pad_ref, 0, z, False)
-        ey = dy(v_ref[1, z], hy, False)
+        ey = y_ref[1, z]
         ez = dz(v_ref, 2, z, layers, False, edge)
         new = (
             s_ref[0, z] + (mod * ex + lam * (ey + ez)),
             s_ref[1, z] + mu * (dz(v_ref, 0, z, layers, True, edge) + dx(pad_ref, 2, z, True)),
-            s_ref[2, z] + mu * (dy(v_ref[0, z], hx, True) + dx(pad_ref, 1, z, True)),
-            s_ref[3, z] + mu * (dz(v_ref, 1, z, layers, True, edge) + dy(v_ref[2, z], hz, True)),
+            s_ref[2, z] + mu * (y_ref[0, z] + dx(pad_ref, 1, z, True)),
+            s_ref[3, z] + mu * (dz(v_ref, 1, z, layers, True, edge) + y_ref[2, z]),
             s_ref[4, z] + (mod * ey + lam * (ex + ez)),
             s_ref[5, z] + (mod * ez + lam * (ex + ey)),
         )
@@ -228,7 +310,48 @@
                 j, m = slot(0, layers, i)
                 put_y(q_ref, j, m + z, new[c])
 
-    over_layers(layers, body)
+    def prepare(group):
+        fill_pad(flags_ref, v_ref, VS, xb_ref, xa_ref, k0, pad_ref, layers, group)
+        fill_dy(group, v_ref, VS, (1, 0, 1), qm_ref, k0, layers, w_ref, t_ref, y_ref)
+
+    return (layers, copies, results, body, prepare), results
+
+
+def stress_kernel(layers, k0, edges, *refs):
+    arguments, _ = stress_parts(layers, k0, edges, *refs)
+    sweep(*arguments)
+
+
+def stress_pair_kernel(flags_ref, *refs):
+    basin, box, halos, (out_b, out_x), refs = refs[0:3], refs[3:6], refs[6:10], refs[10:12], refs[12:]
+    half = len(refs) // 2
+    basin, results_b = stress_parts(NZ, 0, False, flags_ref, *basin, *halos, out_b, *refs[:half])
+    box, results_x = stress_parts(BZ, 3 * NZ, False, flags_ref, *box, *halos, out_x, *refs[half:])
+    sweep(*basin, finish=False)
+    sweep(*box, finish=False)
+    for results in (results_b, results_x):
+        for n in range(len(results)):
+            wait_group(results, n)
+
+
+def forced_velocity_kernel(first, layers, k0, *refs):
+    n = 8 if first else 9
+    force_in, vel_in, refs = refs[:n], refs[n : n + 11], refs[n + 11 :]
+    vel_out, refs = refs[:4], refs[4:]
+    current, refs = (refs[:1], refs[1:]) if first else ((), refs)
+    force_ref, force_scratch, vel_scratch = refs[0], refs[1:5], refs[5:]
+    vel_kernel(
+        layers,
+        k0,
+        True,
+        True,
+        *vel_in[:8],
+        force_ref,
+        *vel_in[8:],
+        *vel_out,
+        *vel_scratch,
+        before=lambda: force_kernel(first, *force_in, force_ref, *current, *force_scratch),
+    )
 
 
 def row_lookup(idx_row):
@@ -292,19 +415,60 @@
     return tiles
 
 
+def inverse_kernel(keys_ref, inv_ref):
+    row = lax.broadcasted_iota(jnp.int32, (GROUPS, BLK), 0)
+    column = lax.broadcasted_iota(jnp.int32, (BLK, BLK), 0)
+    lane = lax.broadcasted_iota(jnp.int32, (GROUPS, BLK), 1).astype(F32)
+
+    def body(b, total):
+        parts, hots = [], []
+        for u in range(8):
+            g = b * 8 + u
+            place = keys_ref[pl.ds(g, 1), :] & (GROUPS * BLK - 1)
+            hit = row == (place >> 7)
+            where_to = jnp.where(hit, lane, 0.0)
+            parts.append(jnp.concatenate([where_to, jnp.where(hit, g.astype(F32), 0.0)], axis=0).astype(BF16))
+            hots.append(jnp.where(column == (place & (BLK - 1)), 1.0, 0.0).astype(BF16))
+        return total + lax.dot_general(
+            jnp.concatenate(parts, axis=1),
+            jnp.concatenate(hots, axis=1),
+            (((1,), (1,)), ((), ())),
+            preferred_element_type=F32,
+        )
+
+    total = lax.fori_loop(0, GROUPS // 8, body, jnp.zeros((2 * GROUPS, BLK), F32))
+    inv_ref[...] = (total[0:GROUPS] + total[GROUPS:] * BLK).astype(jnp.int32)
+
+
 def force_kernel(first, *refs):
-    lo_ref, hi_ref, rs_ref, ys_ref, inv_ref, v_ref, stiff_ref, mass_ref = refs[:8]
+    lo_ref, hi_ref, rs_ref, ys_ref, inv_ref, v_ref, hbm_stiff, hbm_mass = refs[:8]
     refs = refs[8:]
     if not first:
         prev_ref, refs = refs[0], refs[1:]
     force_ref, refs = refs[0], refs[1:]
     if first:
         cur_ref, refs = refs[0], refs[1:]
-    (sorted_ref,) = refs
+    sorted_ref, stiff_ref, mass_ref, sem_ref = refs
+    several = 8
+
+    def matrices(b):
+        part = pl.ds(b * several, several)
+        return [
+            pltpu.make_async_copy(src.at[part], dst.at[part], sem_ref.at[i, b])
+            for i, (src, dst) in enumerate(((hbm_stiff, stiff_ref), (hbm_mass, mass_ref)))
+        ]
+
+    def fetch(b, _):
+        for copy in matrices(b):
+            copy.start()
+        return 0
+
+    lax.fori_loop(0, GROUPS // several, fetch, 0)
     select_sorted(lo_ref, hi_ref, rs_ref, ys_ref, v_ref, sorted_ref)
-    several = 4
 
     def body(b, _):
+        for copy in matrices(b):
+            copy.wait()
         for u in range(several):
             g = b * several + u
             tiles = unsort(sorted_ref, inv_ref, g)
@@ -348,19 +512,33 @@
     return (sds((k, 2, CY)), sds((k, 2, CY)), sds((-(-k // 32), CX, CY)))
 
 
-def velocity_step(name, flags, v, s, media, halos, k0, force=None, carry=()):
+def scratch(layers, q_shape, medias, results):
+    n = len(groups_of(layers))
+    return [
+        pltpu.VMEM((3, layers, CX + 16, CY), F32),
+        pltpu.VMEM(q_shape, F32),
+        pltpu.VMEM((2, 4 * CY, CY), BF16),
+        pltpu.VMEM((3, 4 * CX, 4 * CY), BF16),
+        pltpu.VMEM((3, layers, CX, CY), F32),
+        *(pltpu.VMEM((c, layers, CX, CY), F32) for c in (3, 6, medias, results)),
+        pltpu.SemaphoreType.DMA((3, n)),
+        pltpu.SemaphoreType.DMA((1, n)),
+    ]
+
+
+def velocity_step(name, flags, v, s, media, halos, k0, tiles, sent):
     layers = v.shape[1]
     out = pl.pallas_call(
-        functools.partial(vel_kernel, layers, k0, force is not None, bool(carry)),
-        out_shape=(sds(v.shape), *edge_shapes(layers + (carry[0].shape[0] // 3 if carry else 0))),
-        in_specs=[SM] + [VM] * (7 + (force is not None) + len(carry)),
-        out_specs=(VM,) * 4,
-        scratch_shapes=[pltpu.VMEM((3, layers, CX + 16, CY), F32), pltpu.VMEM(halos[2].shape, F32)],
+        functools.partial(vel_kernel, layers, k0, False, False, sent=sent),
+        out_shape=(sds(v.shape), *edge_shapes(layers), sds((tiles, sent, CX, CY))),
+        in_specs=[SM] + [HB] * 3 + [VM] * 4,
+        out_specs=(HB, VM, VM, VM, HB),
+        scratch_shapes=[*scratch(layers, halos[2].shape, 1, 3), pltpu.SemaphoreType.DMA((2, tiles))],
         compiler_params=PARAMS,
         name=name,
         cost_estimate=cost(60 * v.size, 16 * v.size),
-    )(flags, v, s, media, *halos, *(() if force is None else (force,)), *carry)
-    return out[0], out[1:]
+    )(flags, v, s, media, *halos)
+    return out[0], out[1:4], out[4]
 
 
 def stress_step(name, flags, v, s, media, halos, k0, edges):
@@ -368,9 +546,9 @@
     out = pl.pallas_call(
         functools.partial(stress_kernel, layers, k0, edges),
         out_shape=(sds(s.shape), *(edge_shapes(layers) if edges else ())),
-        in_specs=[SM] + [VM] * 7,
-        out_specs=(VM,) * (4 if edges else 1),
-        scratch_shapes=[pltpu.VMEM((3, layers, CX + 16, CY), F32), pltpu.VMEM(halos[2].shape, F32)],
+        in_specs=[SM] + [HB] * 3 + [VM] * 4,
+        out_specs=(HB, VM, VM, VM) if edges else (HB,),
+        scratch_shapes=scratch(layers, halos[2].shape, 2, 6),
         compiler_params=PARAMS,
         name=name,
         cost_estimate=cost(60 * v.size, 16 * v.size),
@@ -386,13 +564,19 @@
     flags = jnp.stack([gx > 0, gx < nx - 1, gy > 0, gy < ny - 1]).astype(jnp.int32)
 
     def spread(layer):
-        return lax.all_to_all(jnp.broadcast_to(layer[None], (ny, *layer.shape)), "gy", 0, 0, tiled=True)
+        return lax.all_to_all(layer, "gy", 0, 0, tiled=True)
 
     *edges, box_media = pl.pallas_call(
         pack_kernel,
         out_shape=(*edge_shapes(NZ + BZ), sds((3, BZ, CX, CY))),
-        in_specs=[SM, VM, VM, VM],
+        in_specs=[SM, HB, HB, VM],
         out_specs=(VM,) * 4,
+        scratch_shapes=[
+            pltpu.VMEM((5, NZ, CX, CY), F32),
+            pltpu.VMEM((5, BZ, CX, CY), F32),
+            pltpu.SemaphoreType.DMA((1, NZ // 4)),
+            pltpu.SemaphoreType.DMA((1, BZ // 4)),
+        ],
         compiler_params=PARAMS,
         name="pack",
         cost_estimate=cost(2**20, 2**22),
@@ -405,43 +589,78 @@
     keys = lax.sort((own_tile * (CX * CY) + own_cell) * (GROUPS * BLK) + requests)
     rows = (keys >> 20).reshape(GROUPS, BLK)
     cols = ((keys >> 13) & (CY - 1)).reshape(GROUPS, BLK)
-    inverse = lax.sort(((keys & 8191) << 13) | requests)
-    inverse = (inverse & 8191).reshape(GROUPS, BLK)
+    inverse = pl.pallas_call(
+        inverse_kernel,
+        out_shape=sds((GROUPS, BLK), jnp.int32),
+        in_specs=[VM],
+        out_specs=VM,
+        compiler_params=PARAMS,
+        name="inverse",
+        cost_estimate=cost(2**27, 2**16),
+    )(keys.reshape(GROUPS, BLK))
     first, last = rows[:, 0] >> 3, rows[:, BLK - 1] >> 3
     lookup = (first, last, rows, cols, inverse)
 
-    def forces(name, layers, previous):
+    def forced_velocity(name, layers, previous, v, s, media, halos, k0, carry):
         first = previous is None
-        comps = layers.shape[1]
-        shapes = (sds((3, CX, CY)), sds((GROUPS, 8, BLK)))
+        depth = v.shape[1]
+        shapes = (sds(v.shape), *edge_shapes(depth + carry[0].shape[0] // 3), sds((GROUPS, 8, BLK)))
         return pl.pallas_call(
-            functools.partial(force_kernel, first),
-            out_shape=shapes if first else shapes[:1],
-            in_specs=[SM, SM] + [VM] * (6 if first else 7),
-            out_specs=(VM, VM) if first else (VM,),
-            scratch_shapes=[pltpu.VMEM((comps, GROUPS, BLK), F32)],
+            functools.partial(forced_velocity_kernel, first, depth, k0),
+            out_shape=shapes if first else shapes[:4],
+            in_specs=[SM, SM] + [VM] * 4 + [HB] * 2 + [VM] * (not first) + [SM] + [HB] * 3 + [VM] * 7,
+            out_specs=(HB, VM, VM, VM, VM) if first else (HB, VM, VM, VM),
+            scratch_shapes=[
+                pltpu.VMEM((3, CX, CY), F32),
+                pltpu.VMEM((layers.shape[1], GROUPS, BLK), F32),
+                pltpu.VMEM((GROUPS, BLK, BLK), F32),
+                pltpu.VMEM((GROUPS, BLK, BLK), F32),
+                pltpu.SemaphoreType.DMA((2, GROUPS // 8)),
+                *scratch(depth, halos[2].shape, 1, 3),
+            ],
             compiler_params=PARAMS,
             name=name,
-            cost_estimate=cost(2**30, 2**23),
-        )(*lookup, layers, drm_stiff[0, 0], drm_mass[0, 0], *(() if first else (previous,)))
-
-    layer0 = basin_v[:, ZR]
-    basin_v, edges_b = velocity_step("basin_v1", flags, basin_v, basin_s, basin_media, halos, 0)
-    layers01 = spread(jnp.concatenate([layer0, basin_v[:, ZR]]))
+            cost_estimate=cost(2**30, 2**24),
+        )(
+            *lookup,
+            layers,
+            drm_stiff[0, 0],
+            drm_mass[0, 0],
+            *(() if first else (previous,)),
+            flags,
+            v,
+            s,
+            media,
+            *halos,
+            *carry,
+        )
+
+    basin_v, edges_b, layers01 = velocity_step(
+        "basin_v1", flags, basin_v, basin_s, basin_media, halos, 0, ny, 6
+    )
+    layers01 = spread(layers01)
     halos_b = trade(edges_b)
     basin_s, edges_b = stress_step("basin_s1", flags, basin_v, basin_s, basin_media, halos_b, 0, True)
-    force, current = forces("force1", layers01, None)
-    box_v, edges = velocity_step("box_v1", flags, box_v, box_s, box_media, halos, 3 * NZ, force, edges_b)
+    box_v, *edges, current = forced_velocity(
+        "box_v1", layers01, None, box_v, box_s, box_media, halos, 3 * NZ, edges_b
+    )
     halos = trade(edges)
-    basin_v, edges_b = velocity_step("basin_v2", flags, basin_v, basin_s, basin_media, halos, 0)
-    layer2 = spread(basin_v[:, ZR])
+    basin_v, edges_b, layer2 = velocity_step("basin_v2", flags, basin_v, basin_s, basin_media, halos, 0, ny, 3)
+    layer2 = spread(layer2)
     box_s, edges_x = stress_step("box_s1", flags, box_v, box_s, box_media, halos, 3 * NZ, True)
     halos_x = trade(edges_x)
-    (force,) = forces("force2", layer2, current)
-    box_v, edges = velocity_step("box_v2", flags, box_v, box_s, box_media, halos_x, 0, force, edges_b)
+    box_v, *edges = forced_velocity("box_v2", layer2, current, box_v, box_s, box_media, halos_x, 0, edges_b)
     halos = trade(edges)
-    basin_s, _ = stress_step("basin_s2", flags, basin_v, basin_s, basin_media, halos, 0, False)
-    box_s, _ = stress_step("box_s2", flags, box_v, box_s, box_media, halos, 3 * NZ, False)
+    basin_s, box_s = pl.pallas_call(
+        stress_pair_kernel,
+        out_shape=(sds(basin_s.shape), sds(box_s.shape)),
+        in_specs=[SM] + [HB] * 6 + [VM] * 4,
+        out_specs=(HB, HB),
+        scratch_shapes=[*scratch(NZ, halos[2].shape, 2, 6), *scratch(BZ, halos[2].shape, 2, 6)],
+        compiler_params=PARAMS,
+        name="stress2",
+        cost_estimate=cost(2**26, 2**24),
+    )(flags, basin_v, basin_s, basin_media, box_v, box_s, box_media, *halos)
     return basin_v, basin_s, box_v, box_s
 
 

time: 204 us -> 167 us (0.82)
  local copies, waits for them, and re-layouts: 41.3 us -> 4.63 us
  other arithmetic: 19.5 us -> 9.56 us
  Pallas kernels: 67.9 us -> 75.9 us
    unnamed x120 -> x56, local copies, waits for them, and re-layouts: 37.5 us -> 4.6 us
    pallas_call x6, Pallas kernels: 45.4 us -> 56.3 us  [the longest x2 28.5 us: forced_velocity(): pl.pallas_call(functools.partial(forced_velocity_kernel, first, depth, k0...]
    sort x1 -> x0, other arithmetic: 7.54 us -> none  [shards(): inverse = lax.sort((keys & 8191) << 13 | requests)]
    pallas_call x4 -> x2, Pallas kernels: 18.7 us -> 14.3 us  [stress_step(): pl.pallas_call(functools.partial(stress_kernel, layers, k0, edges), out_s...]
    broadcast_in_dim x3 -> x0, local copies, waits for them, and re-layouts: 3.21 us -> none  [spread(): jnp.broadcast_to(layer[None], (ny, *layer.shape))]
  transfers between devices with their start and end apart: 22 -> 22, of which waited for: 8 -> 11; matrix products, arithmetic and copies ran while one was open for 10% -> 6% of each run, Pallas kernels for 10% -> 11%
where the time goes in v2:
time: 167 us; the launch traced here: 166 us
  Pallas kernels  75.9 us (45%)
  starting transfers between devices  56.2 us (34%)
  waiting for transfers between devices  18.6 us (11%)
  other arithmetic  9.56 us (6%)
  local copies, waits for them, and re-layouts  4.63 us (3%)
    ppermute x20, starting transfers between devices, ring(): return lax.ppermute(value, axis, [(i, (i + step) % n) for i in range(n)])  45 us
    pallas_call x2, Pallas kernels, forced_velocity(): pl.pallas_call(functools.partial(forced_velocity_kernel, first, depth, k0...  28.5 us
    ppermute x20, waiting for transfers between devices, ring(): return lax.ppermute(value, axis, [(i, (i + step) % n) for i in range(n)])  18.6 us
    pallas_call x2, Pallas kernels, velocity_step(): pl.pallas_call(functools.partial(vel_kernel, layers, k0, False, False, se...  15.9 us
    pallas_call x2, Pallas kernels, stress_step(): pl.pallas_call(functools.partial(stress_kernel, layers, k0, edges), out_s...  14.3 us
    all_to_all x2, starting transfers between devices, spread(): return lax.all_to_all(layer, 'gy', 0, 0, tiled=True)  11.2 us
    pallas_call x1, Pallas kernels, shards(): pl.pallas_call(stress_pair_kernel, out_shape=(sds(basin_s.shape), sds(box...  8.52 us
    sort x1, other arithmetic, shards(): lax.sort((own_tile * (CX * CY) + own_cell) * (GROUPS * BLK) + requests)  6.77 us
  transfers between devices with their start and end apart: 22, of which 11 were waited for; matrix products, arithmetic and copies ran while one was open for 6% of the time, Pallas kernels for 11%

profile of v2, /device:TPU:0, one launch (start us, length us, event | category | flops | bytes accessed | tf_op | source)
XLA Modules:
  0.0 166.0 jit_solution(2490931552355424782)
XLA Ops:
  0.6 0.0 copy-start
  0.6 5.3 %pack.1 = (f32[72,2,128]{2,1,0:T(2,128)}, f32[72,2,128]{2,1,0:T(2,128)}, f32[3,64,128]{2,1,0:T(8,128)}, f32[3,8,64,128]{3,2,1,0:T(8,128)}) custom-call(f32[3,8]{1,0:T(4,128)} %zm_ref.1, f32[6,16,64,128]{3,2,1,0:T(8,128)} %refs_2_.5, f32[6,8,64,128]{3,2,1,0:T(8,128)} %refs_2_.6, s32[8,64,128]{2,1,0:T(8,128)} %ids_ref.1), custom_call_target="tpu_custom_call" | custom-call | flops 1048576 | bytes 4194304 | tf_op jit(solution)/shard_map/pack/pallas_call | solution.py:569
  6.0 5.6 %collective-permute-start.3 = (f32[3,64,128]{2,1,0:T(8,128)}, f32[3,64,128]{2,1,0:T(8,128)S(1)}, u32[]{:S(2)}, u32[]{:S(2)}) collective-permute-start(f32[3,64,128]{2,1,0:T(8,128)} %get-tuple-element.41), channel_id=1, source_target_pairs={{0,7},{1,0},{2,1},{3,2},{4,3},{5,4},{6,5},{7,6},{8,15},{9,8},{10,9... | collective-permute-start | bytes 294920 | tf_op jit(solution)/shard_map/ppermute | solution.py:498
  11.6 3.9 %collective-permute-start.1 = (f32[72,2,128]{2,1,0:T(2,128)}, f32[72,2,128]{2,1,0:T(2,128)S(1)}, u32[]{:S(2)}, u32[]{:S(2)}) collective-permute-start(f32[72,2,128]{2,1,0:T(2,128)} %get-tuple-element.40), channel_id=1, source_target_pairs={{0,120},{8,0},{16,8},{24,16},{32,24},{40,32},{48,40},{56,48},{64,5... | collective-permute-start | bytes 221192 | tf_op jit(solution)/shard_map/ppermute | solution.py:498
  15.5 0.8 dynamic-slice_multiply_fusion
  16.2 0.6 add_convert_fusion.refs_0_.refs_8_.refs_9_.flags_ref
  16.9 2.0 %collective-permute-done.refs_4_.refs_12_ = f32[72,2,128]{2,1,0:T(2,128)S(1)} collective-permute-done((f32[72,2,128]{2,1,0:T(2,128)}, f32[72,2,128]{2,1,0:T(2,128)S(1)}, u32[]{:S(2)}, u32[]{:S(2)}) %collective-permute-start) | collective-permute-done | bytes 73760 | tf_op jit(solution)/shard_map/ppermute | solution.py:498
  18.8 1.2 collective-permute-done.2.refs_6_.refs_14_
  20.1 0.6 copy-done.5
  20.7 8.0 %basin_v1.1 = (f32[3,16,64,128]{3,2,1,0:T(8,128)}, f32[48,2,128]{2,1,0:T(2,128)}, f32[48,2,128]{2,1,0:T(2,128)}, f32[2,64,128]{2,1,0:T(8,128)}, f32[8,6,64,128]{3,2,1,0:T(8,128)}) custom-call(s32[4]{0:T(128)} %add_convert_fusion.refs_0_.refs_8_.refs_9_.flags_ref, f32[3,16,64,128]{3,2,1,0:T(8,128)} %refs_1_.1, f32[6,16,64,128]{3,2,1,0:T(8,128)} %refs_2_.5, ...), custom_call_target="tpu_custom_call" | custom-call | flops 23592960 | bytes 6291456 | tf_op jit(solution)/shard_map/basin_v1/pallas_call | solution.py:531
  28.7 0.0 copy-start.25
  28.7 6.5 %all-to-all-start = ((f32[8,6,64,128]{3,2,1,0:T(8,128)}), f32[8,6,64,128]{3,2,1,0:T(8,128)S(1)}, u32[]{:S(2)}, u32[]{:S(2)}) async-start(f32[8,6,64,128]{3,2,1,0:T(8,128)} %get-tuple-element.48), calls=%async_computation | async-start | bytes 3145728 | tf_op jit(solution)/shard_map/all_to_all | solution.py:567
  35.3 6.8 %sort.14 = (s32[8192]{0:T(1024)S(1)}, s32[8192]{0:T(1024)}) sort(s32[8192]{0:T(1024)S(1)} %iota_add_fusion, s32[8192]{0:T(1024)S(1)} %iota.7), dimensions={0}, to_apply=%region_0.1 | sort | flops 106496 | bytes 131072 | tf_op jit(solution)/shard_map/sort | solution.py:589
  42.0 0.6 and_bitcast_fusion
  42.7 5.6 %collective-permute-start.7 = (f32[2,64,128]{2,1,0:T(8,128)S(1)}, f32[2,64,128]{2,1,0:T(8,128)S(1)}, u32[]{:S(2)}, u32[]{:S(2)}) collective-permute-start(f32[2,64,128]{2,1,0:T(8,128)S(1)} %copy-done.25), channel_id=1, source_target_pairs={{0,7},{1,0},{2,1},{3,2},{4,3},{5,4},{6,5},{7,6},{8,15},{9,8},{10,9... | collective-permute-start | bytes 196616 | tf_op jit(solution)/shard_map/ppermute | solution.py:498
  48.3 3.8 %collective-permute-start.5 = (f32[48,2,128]{2,1,0:T(2,128)S(1)}, f32[48,2,128]{2,1,0:T(2,128)S(1)}, u32[]{:S(2)}, u32[]{:S(2)}) collective-permute-start(f32[48,2,128]{2,1,0:T(2,128)S(1)} %copy-done.26), channel_id=1, source_target_pairs={{0,120},{8,0},{16,8},{24,16},{32,24},{40,32},{48,40},{56,48},{64,5... | collective-permute-start | bytes 147464 | tf_op jit(solution)/shard_map/ppermute | solution.py:498
  52.2 0.8 fusion
  52.9 3.4 %inverse.1.refs_4_ = s32[64,128]{1,0:T(8,128)} custom-call(s32[64,128]{1,0:T(8,128)} %bitcast.19), custom_call_target="tpu_custom_call" | custom-call | flops 134217728 | bytes 65536 | tf_op jit(solution)/shard_map/inverse/pallas_call | solution.py:592
  56.3 1.0 collective-permute-done.4.refs_4_
  57.3 1.4 collective-permute-done.6.refs_6_
  58.7 0.6 copy-done.17
  59.3 8.2 %basin_s1.1 = (f32[6,16,64,128]{3,2,1,0:T(8,128)}, f32[48,2,128]{2,1,0:T(2,128)}, f32[48,2,128]{2,1,0:T(2,128)}, f32[2,64,128]{2,1,0:T(8,128)}) custom-call(s32[4]{0:T(128)} %add_convert_fusion.refs_0_.refs_8_.refs_9_.flags_ref, f32[3,16,64,128]{3,2,1,0:T(8,128)} %get-tuple-element.42.refs_1_, f32[6,16,64,128]{3,2,1,0:T(8,128)} %refs_2_.5, ...), custom_call_target="tpu_custom_call" | custom-call | flops 23592960 | bytes 6291456 | tf_op jit(solution)/shard_map/basin_s1/pallas_call | solution.py:546
  67.6 0.0 copy-start.1
  67.6 1.1 copy-done.1
  68.7 15.6 %box_v1.1 = (f32[3,8,64,128]{3,2,1,0:T(8,128)}, f32[72,2,128]{2,1,0:T(2,128)}, f32[72,2,128]{2,1,0:T(2,128)}, f32[3,64,128]{2,1,0:T(8,128)}, f32[64,8,128]{2,1,0:T(8,128)}) custom-call(s32[64]{0:T(128)} %get-tuple-element.74.refs_0_, s32[64]{0:T(128)} %get-tuple-element.73.refs_1_, s32[64,128]{1,0:T(8,128)} %copy-done.3, ...), custom_call_target="tpu_custom_call" | custom-call | flops 1073741824 | bytes 16777216 | tf_op jit(solution)/shard_map/box_v1/pallas_call | solution.py:608
  84.4 5.1 %collective-permute-start.11 = (f32[3,64,128]{2,1,0:T(8,128)}, f32[3,64,128]{2,1,0:T(8,128)S(1)}, u32[]{:S(2)}, u32[]{:S(2)}) collective-permute-start(f32[3,64,128]{2,1,0:T(8,128)} %get-tuple-element.55), channel_id=1, source_target_pairs={{0,7},{1,0},{2,1},{3,2},{4,3},{5,4},{6,5},{7,6},{8,15},{9,8},{10,9... | collective-permute-start | bytes 294920 | tf_op jit(solution)/shard_map/ppermute | solution.py:498
  89.5 3.9 %collective-permute-start.9 = (f32[72,2,128]{2,1,0:T(2,128)}, f32[72,2,128]{2,1,0:T(2,128)S(1)}, u32[]{:S(2)}, u32[]{:S(2)}) collective-permute-start(f32[72,2,128]{2,1,0:T(2,128)} %get-tuple-element.54), channel_id=1, source_target_pairs={{0,120},{8,0},{16,8},{24,16},{32,24},{40,32},{48,40},{56,48},{64,5... | collective-permute-start | bytes 221192 | tf_op jit(solution)/shard_map/ppermute | solution.py:498
  93.3 2.2 %collective-permute-done.8.refs_4_ = f32[72,2,128]{2,1,0:T(2,128)S(1)} collective-permute-done((f32[72,2,128]{2,1,0:T(2,128)}, f32[72,2,128]{2,1,0:T(2,128)S(1)}, u32[]{:S(2)}, u32[]{:S(2)}) %collective-permute-start.8) | collective-permute-done | bytes 73760 | tf_op jit(solution)/shard_map/ppermute | solution.py:498
  95.6 0.1 collective-permute-done.9.refs_5_
  95.6 2.3 %collective-permute-done.10.refs_6_ = f32[3,64,128]{2,1,0:T(8,128)S(1)} collective-permute-done((f32[3,64,128]{2,1,0:T(8,128)}, f32[3,64,128]{2,1,0:T(8,128)S(1)}, u32[]{:S(2)}, u32[]{:S(2)}) %collective-permute-start.10) | collective-permute-done | bytes 98336 | tf_op jit(solution)/shard_map/ppermute | solution.py:498
  97.9 0.6 copy-done.7
  98.6 8.0 %basin_v2.1 = (f32[3,16,64,128]{3,2,1,0:T(8,128)}, f32[48,2,128]{2,1,0:T(2,128)}, f32[48,2,128]{2,1,0:T(2,128)}, f32[2,64,128]{2,1,0:T(8,128)}, f32[8,3,64,128]{3,2,1,0:T(8,128)}) custom-call(s32[4]{0:T(128)} %add_convert_fusion.refs_0_.refs_8_.refs_9_.flags_ref, f32[3,16,64,128]{3,2,1,0:T(8,128)} %get-tuple-element.42.refs_1_, ...), custom_call_target="tpu_custom_call" | custom-call | flops 23592960 | bytes 6291456 | tf_op jit(solution)/shard_map/basin_v2/pallas_call | solution.py:531
  106.5 4.7 %all-to-all-start.1 = ((f32[8,3,64,128]{3,2,1,0:T(8,128)}), f32[8,3,64,128]{3,2,1,0:T(8,128)S(1)}, u32[]{:S(2)}, u32[]{:S(2)}) async-start(f32[8,3,64,128]{3,2,1,0:T(8,128)} %get-tuple-element.57), calls=%async_computation.1 | async-start | bytes 1572864 | tf_op jit(solution)/shard_map/all_to_all | solution.py:567
  111.3 6.1 %box_s1.1 = (f32[6,8,64,128]{3,2,1,0:T(8,128)}, f32[24,2,128]{2,1,0:T(2,128)}, f32[24,2,128]{2,1,0:T(2,128)}, f32[1,64,128]{2,1,0:T(8,128)}) custom-call(s32[4]{0:T(128)} %add_convert_fusion.refs_0_.refs_8_.refs_9_.flags_ref, f32[3,8,64,128]{3,2,1,0:T(8,128)} %get-tuple-element.59.refs_1_.refs_10_, f32[6,8,64,128]{3,2,1,0:T(8,128)} %refs_2_.6, ...), custom_call_target="tpu_custom_call" | custom-call | flops 11796480 | bytes 3145728 | tf_op jit(solution)/shard_map/box_s1/pallas_call | solution.py:546
  117.4 5.7 %collective-permute-start.15 = (f32[1,64,128]{2,1,0:T(8,128)}, f32[1,64,128]{2,1,0:T(8,128)S(1)}, u32[]{:S(2)}, u32[]{:S(2)}) collective-permute-start(f32[1,64,128]{2,1,0:T(8,128)} %get-tuple-element.63), channel_id=1, source_target_pairs={{0,7},{1,0},{2,1},{3,2},{4,3},{5,4},{6,5},{7,6},{8,15},{9,8},{10,9... | collective-permute-start | bytes 98312 | tf_op jit(solution)/shard_map/ppermute | solution.py:498
  123.1 3.9 %collective-permute-start.13 = (f32[24,2,128]{2,1,0:T(2,128)}, f32[24,2,128]{2,1,0:T(2,128)S(1)}, u32[]{:S(2)}, u32[]{:S(2)}) collective-permute-start(f32[24,2,128]{2,1,0:T(2,128)} %get-tuple-element.62), channel_id=1, source_target_pairs={{0,120},{8,0},{16,8},{24,16},{32,24},{40,32},{48,40},{56,48},{64,5... | collective-permute-start | bytes 73736 | tf_op jit(solution)/shard_map/ppermute | solution.py:498
  126.9 1.7 %collective-permute-done.12.refs_13_ = f32[24,2,128]{2,1,0:T(2,128)S(1)} collective-permute-done((f32[24,2,128]{2,1,0:T(2,128)}, f32[24,2,128]{2,1,0:T(2,128)S(1)}, u32[]{:S(2)}, u32[]{:S(2)}) %collective-permute-start.12) | collective-permute-done | bytes 24608 | tf_op jit(solution)/shard_map/ppermute | solution.py:498
  128.6 0.0 collective-permute-done.13.refs_14_
  128.7 2.1 %collective-permute-done.14.refs_15_ = f32[1,64,128]{2,1,0:T(8,128)S(1)} collective-permute-done((f32[1,64,128]{2,1,0:T(8,128)}, f32[1,64,128]{2,1,0:T(8,128)S(1)}, u32[]{:S(2)}, u32[]{:S(2)}) %collective-permute-start.14) | collective-permute-done | bytes 32800 | tf_op jit(solution)/shard_map/ppermute | solution.py:498
  130.8 0.6 copy-done.21
  131.4 0.3 copy-done.2
  131.7 12.9 %box_v2.1 = (f32[3,8,64,128]{3,2,1,0:T(8,128)}, f32[72,2,128]{2,1,0:T(2,128)}, f32[72,2,128]{2,1,0:T(2,128)}, f32[3,64,128]{2,1,0:T(8,128)}) custom-call(s32[64]{0:T(128)} %get-tuple-element.74.refs_0_, s32[64]{0:T(128)} %get-tuple-element.73.refs_1_, s32[64,128]{1,0:T(8,128)} %copy-done.3, s32[64,128]{1,0:T(8,128)} %get-tuple-element.75.refs_3_, ...), custom_call_target="tpu_custom_call" | custom-call | flops 1073741824 | bytes 16777216 | tf_op jit(solution)/shard_map/box_v2/pallas_call | solution.py:608
  144.6 3.7 %collective-permute-start.19 = (f32[3,64,128]{2,1,0:T(8,128)}, f32[3,64,128]{2,1,0:T(8,128)S(1)}, u32[]{:S(2)}, u32[]{:S(2)}) collective-permute-start(f32[3,64,128]{2,1,0:T(8,128)} %get-tuple-element.70), channel_id=1, source_target_pairs={{0,7},{1,0},{2,1},{3,2},{4,3},{5,4},{6,5},{7,6},{8,15},{9,8},{10,9... | collective-permute-start | bytes 294920 | tf_op jit(solution)/shard_map/ppermute | solution.py:498
  148.2 3.9 %collective-permute-start.17 = (f32[72,2,128]{2,1,0:T(2,128)}, f32[72,2,128]{2,1,0:T(2,128)S(1)}, u32[]{:S(2)}, u32[]{:S(2)}) collective-permute-start(f32[72,2,128]{2,1,0:T(2,128)} %get-tuple-element.69), channel_id=1, source_target_pairs={{0,120},{8,0},{16,8},{24,16},{32,24},{40,32},{48,40},{56,48},{64,5... | collective-permute-start | bytes 221192 | tf_op jit(solution)/shard_map/ppermute | solution.py:498
  152.1 2.5 %collective-permute-done.16.refs_6_ = f32[72,2,128]{2,1,0:T(2,128)S(1)} collective-permute-done((f32[72,2,128]{2,1,0:T(2,128)}, f32[72,2,128]{2,1,0:T(2,128)S(1)}, u32[]{:S(2)}, u32[]{:S(2)}) %collective-permute-start.16) | collective-permute-done | bytes 73760 | tf_op jit(solution)/shard_map/ppermute | solution.py:498
  154.6 2.1 %collective-permute-done.18.refs_8_ = f32[3,64,128]{2,1,0:T(8,128)S(1)} collective-permute-done((f32[3,64,128]{2,1,0:T(8,128)}, f32[3,64,128]{2,1,0:T(8,128)S(1)}, u32[]{:S(2)}, u32[]{:S(2)}) %collective-permute-start.18) | collective-permute-done | bytes 98336 | tf_op jit(solution)/shard_map/ppermute | solution.py:498
  156.7 0.6 copy-done.13
  157.3 8.5 %stress2.1 = (f32[6,16,64,128]{3,2,1,0:T(8,128)}, f32[6,8,64,128]{3,2,1,0:T(8,128)}) custom-call(s32[4]{0:T(128)} %add_convert_fusion.refs_0_.refs_8_.refs_9_.flags_ref, f32[3,16,64,128]{3,2,1,0:T(8,128)} %get-tuple-element.35.refs_0_, f32[6,16,64,128]{3,2,1,0:T(8,128)} %get-tuple-element.46.refs_2_.refs_1_, f32[3,16,64,128]{3,2,1,0:T(8,128)} %refs_2_.7, ...), custom_call_target="tpu_custom_call" | custom-call | flops 67108864 | bytes 16777216 | tf_op jit(solution)/shard_map/stress2/pallas_call | solution.py:654
  (69 shorter events, 0.2 us)
Async XLA Ops:
  0.6 34.6 %copy-start = (s32[1,8,8192]{2,1,0:T(8,128)S(1)}, s32[1,8,8192]{2,1,0:T(8,128)}, u32[]{:S(2)}) copy-start(s32[1,8,8192]{2,1,0:T(8,128)} %param.19) | copy-start | bytes 786436
  6.0 12.8 %collective-permute-start.3 = (f32[3,64,128]{2,1,0:T(8,128)}, f32[3,64,128]{2,1,0:T(8,128)S(1)}, u32[]{:S(2)}, u32[]{:S(2)}) collective-permute-start(f32[3,64,128]{2,1,0:T(8,128)} %get-tuple-element.41), channel_id=1, source_target_pairs={{0,7},{1,0},{2,1},{3,2},{4,3},{5,4},{6,5},{7,6},{8,15},{9,8},{10,9... | collective-permute-start | bytes 294920 | tf_op jit(solution)/shard_map/ppermute | solution.py:498
  11.6 8.4 %collective-permute-start.2 = (f32[3,64,128]{2,1,0:T(8,128)}, f32[3,64,128]{2,1,0:T(8,128)S(1)}, u32[]{:S(2)}, u32[]{:S(2)}) collective-permute-start(f32[3,64,128]{2,1,0:T(8,128)} %get-tuple-element.41), channel_id=1, source_target_pairs={{0,1},{1,2},{2,3},{3,4},{4,5},{5,6},{6,7},{7,0},{8,9},{9,10},{10,1... | collective-permute-start | bytes 294920 | tf_op jit(solution)/shard_map/ppermute | solution.py:498
  11.6 7.2 %collective-permute-start = (f32[72,2,128]{2,1,0:T(2,128)}, f32[72,2,128]{2,1,0:T(2,128)S(1)}, u32[]{:S(2)}, u32[]{:S(2)}) collective-permute-start(f32[72,2,128]{2,1,0:T(2,128)} %get-tuple-element.39), channel_id=1, source_target_pairs={{0,8},{8,16},{16,24},{24,32},{32,40},{40,48},{48,56},{56,64},{64,7... | collective-permute-start | bytes 221192 | tf_op jit(solution)/shard_map/ppermute | solution.py:498
  11.6 7.2 %collective-permute-start.1 = (f32[72,2,128]{2,1,0:T(2,128)}, f32[72,2,128]{2,1,0:T(2,128)S(1)}, u32[]{:S(2)}, u32[]{:S(2)}) collective-permute-start(f32[72,2,128]{2,1,0:T(2,128)} %get-tuple-element.40), channel_id=1, source_target_pairs={{0,120},{8,0},{16,8},{24,16},{32,24},{40,32},{48,40},{56,48},{64,5... | collective-permute-start | bytes 221192 | tf_op jit(solution)/shard_map/ppermute | solution.py:498
  18.8 1.2 copy-start.10
  18.8 1.2 copy-start.11
  18.8 1.2 copy-start.4
  20.1 0.6 copy-start.5
  28.7 14.0 %copy-start.25 = (f32[2,64,128]{2,1,0:T(8,128)S(1)}, f32[2,64,128]{2,1,0:T(8,128)}, u32[]{:S(2)}) copy-start(f32[2,64,128]{2,1,0:T(8,128)} %get-tuple-element.45) | copy-start | bytes 196612
  28.7 19.6 %copy-start.27 = (f32[48,2,128]{2,1,0:T(2,128)S(1)}, f32[48,2,128]{2,1,0:T(2,128)}, u32[]{:S(2)}) copy-start(f32[48,2,128]{2,1,0:T(2,128)} %get-tuple-element.43) | copy-start | bytes 147460
  28.7 19.6 %copy-start.26 = (f32[48,2,128]{2,1,0:T(2,128)S(1)}, f32[48,2,128]{2,1,0:T(2,128)}, u32[]{:S(2)}) copy-start(f32[48,2,128]{2,1,0:T(2,128)} %get-tuple-element.44) | copy-start | bytes 147460
  28.7 38.9 %all-to-all-start = ((f32[8,6,64,128]{3,2,1,0:T(8,128)}), f32[8,6,64,128]{3,2,1,0:T(8,128)S(1)}, u32[]{:S(2)}, u32[]{:S(2)}) async-start(f32[8,6,64,128]{3,2,1,0:T(8,128)} %get-tuple-element.48), calls=%async_computation | async-start | bytes 3145728 | tf_op jit(solution)/shard_map/all_to_all | solution.py:567
  42.0 10.9 %copy-start.22 = (s32[8192]{0:T(1024)}, s32[8192]{0:T(1024)S(1)}, u32[]{:S(2)}) copy-start(s32[8192]{0:T(1024)S(1)} %get-tuple-element.47) | copy-start | bytes 98308
  42.7 24.9 %copy-start.3 = (s32[64,128]{1,0:T(8,128)}, s32[64,128]{1,0:T(8,128)S(1)}, u32[]{:S(2)}) copy-start(s32[64,128]{1,0:T(8,128)S(1)} %get-tuple-element.76.refs_2_) | copy-start | bytes 98308
  42.7 14.6 %collective-permute-start.7 = (f32[2,64,128]{2,1,0:T(8,128)S(1)}, f32[2,64,128]{2,1,0:T(8,128)S(1)}, u32[]{:S(2)}, u32[]{:S(2)}) collective-permute-start(f32[2,64,128]{2,1,0:T(8,128)S(1)} %copy-done.25), channel_id=1, source_target_pairs={{0,7},{1,0},{2,1},{3,2},{4,3},{5,4},{6,5},{7,6},{8,15},{9,8},{10,9... | collective-permute-start | bytes 196616 | tf_op jit(solution)/shard_map/ppermute | solution.py:498
  48.3 10.4 %collective-permute-start.6 = (f32[2,64,128]{2,1,0:T(8,128)S(1)}, f32[2,64,128]{2,1,0:T(8,128)S(1)}, u32[]{:S(2)}, u32[]{:S(2)}) collective-permute-start(f32[2,64,128]{2,1,0:T(8,128)S(1)} %copy-done.25), channel_id=1, source_target_pairs={{0,1},{1,2},{2,3},{3,4},{4,5},{5,6},{6,7},{7,0},{8,9},{9,10},{10,1... | collective-permute-start | bytes 196616 | tf_op jit(solution)/shard_map/ppermute | solution.py:498
  48.3 9.0 %collective-permute-start.4 = (f32[48,2,128]{2,1,0:T(2,128)S(1)}, f32[48,2,128]{2,1,0:T(2,128)S(1)}, u32[]{:S(2)}, u32[]{:S(2)}) collective-permute-start(f32[48,2,128]{2,1,0:T(2,128)S(1)} %copy-done.27), channel_id=1, source_target_pairs={{0,8},{8,16},{16,24},{24,32},{32,40},{40,48},{48,56},{56,64},{64,7... | collective-permute-start | bytes 147464 | tf_op jit(solution)/shard_map/ppermute | solution.py:498
  48.3 9.0 %collective-permute-start.5 = (f32[48,2,128]{2,1,0:T(2,128)S(1)}, f32[48,2,128]{2,1,0:T(2,128)S(1)}, u32[]{:S(2)}, u32[]{:S(2)}) collective-permute-start(f32[48,2,128]{2,1,0:T(2,128)S(1)} %copy-done.26), channel_id=1, source_target_pairs={{0,120},{8,0},{16,8},{24,16},{32,24},{40,32},{48,40},{56,48},{64,5... | collective-permute-start | bytes 147464 | tf_op jit(solution)/shard_map/ppermute | solution.py:498
  57.3 1.4 copy-start.18
  57.3 1.4 copy-start.19
  57.3 1.4 copy-start.16
  67.6 1.1 copy-start.1
  84.4 11.3 %collective-permute-start.11 = (f32[3,64,128]{2,1,0:T(8,128)}, f32[3,64,128]{2,1,0:T(8,128)S(1)}, u32[]{:S(2)}, u32[]{:S(2)}) collective-permute-start(f32[3,64,128]{2,1,0:T(8,128)} %get-tuple-element.55), channel_id=1, source_target_pairs={{0,7},{1,0},{2,1},{3,2},{4,3},{5,4},{6,5},{7,6},{8,15},{9,8},{10,9... | collective-permute-start | bytes 294920 | tf_op jit(solution)/shard_map/ppermute | solution.py:498
  89.5 8.4 %collective-permute-start.10 = (f32[3,64,128]{2,1,0:T(8,128)}, f32[3,64,128]{2,1,0:T(8,128)S(1)}, u32[]{:S(2)}, u32[]{:S(2)}) collective-permute-start(f32[3,64,128]{2,1,0:T(8,128)} %get-tuple-element.55), channel_id=1, source_target_pairs={{0,1},{1,2},{2,3},{3,4},{4,5},{5,6},{6,7},{7,0},{8,9},{9,10},{10,1... | collective-permute-start | bytes 294920 | tf_op jit(solution)/shard_map/ppermute | solution.py:498
  89.5 6.1 %collective-permute-start.8 = (f32[72,2,128]{2,1,0:T(2,128)}, f32[72,2,128]{2,1,0:T(2,128)S(1)}, u32[]{:S(2)}, u32[]{:S(2)}) collective-permute-start(f32[72,2,128]{2,1,0:T(2,128)} %get-tuple-element.53), channel_id=1, source_target_pairs={{0,8},{8,16},{16,24},{24,32},{32,40},{40,48},{48,56},{56,64},{64,7... | collective-permute-start | bytes 221192 | tf_op jit(solution)/shard_map/ppermute | solution.py:498
  89.5 6.2 %collective-permute-start.9 = (f32[72,2,128]{2,1,0:T(2,128)}, f32[72,2,128]{2,1,0:T(2,128)S(1)}, u32[]{:S(2)}, u32[]{:S(2)}) collective-permute-start(f32[72,2,128]{2,1,0:T(2,128)} %get-tuple-element.54), channel_id=1, source_target_pairs={{0,120},{8,0},{16,8},{24,16},{32,24},{40,32},{48,40},{56,48},{64,5... | collective-permute-start | bytes 221192 | tf_op jit(solution)/shard_map/ppermute | solution.py:498
  95.6 2.3 %copy-start.8 = (f32[72,2,128]{2,1,0:T(2,128)}, f32[72,2,128]{2,1,0:T(2,128)S(1)}, u32[]{:S(2)}) copy-start(f32[72,2,128]{2,1,0:T(2,128)S(1)} %collective-permute-done.8.refs_4_) | copy-start | bytes 221188
  95.6 2.3 %copy-start.9 = (f32[72,2,128]{2,1,0:T(2,128)}, f32[72,2,128]{2,1,0:T(2,128)S(1)}, u32[]{:S(2)}) copy-start(f32[72,2,128]{2,1,0:T(2,128)S(1)} %collective-permute-done.9.refs_5_) | copy-start | bytes 221188
  95.6 2.3 %copy-start.6 = (f32[3,64,128]{2,1,0:T(8,128)}, f32[3,64,128]{2,1,0:T(8,128)S(1)}, u32[]{:S(2)}) copy-start(f32[3,64,128]{2,1,0:T(8,128)S(1)} %collective-permute-done.11.refs_7_) | copy-start | bytes 294916
  97.9 0.6 copy-start.7
  106.5 24.3 %all-to-all-start.1 = ((f32[8,3,64,128]{3,2,1,0:T(8,128)}), f32[8,3,64,128]{3,2,1,0:T(8,128)S(1)}, u32[]{:S(2)}, u32[]{:S(2)}) async-start(f32[8,3,64,128]{3,2,1,0:T(8,128)} %get-tuple-element.57), calls=%async_computation.1 | async-start | bytes 1572864 | tf_op jit(solution)/shard_map/all_to_all | solution.py:567
  117.4 11.3 %collective-permute-start.15 = (f32[1,64,128]{2,1,0:T(8,128)}, f32[1,64,128]{2,1,0:T(8,128)S(1)}, u32[]{:S(2)}, u32[]{:S(2)}) collective-permute-start(f32[1,64,128]{2,1,0:T(8,128)} %get-tuple-element.63), channel_id=1, source_target_pairs={{0,7},{1,0},{2,1},{3,2},{4,3},{5,4},{6,5},{7,6},{8,15},{9,8},{10,9... | collective-permute-start | bytes 98312 | tf_op jit(solution)/shard_map/ppermute | solution.py:498
  123.1 7.7 %collective-permute-start.14 = (f32[1,64,128]{2,1,0:T(8,128)}, f32[1,64,128]{2,1,0:T(8,128)S(1)}, u32[]{:S(2)}, u32[]{:S(2)}) collective-permute-start(f32[1,64,128]{2,1,0:T(8,128)} %get-tuple-element.63), channel_id=1, source_target_pairs={{0,1},{1,2},{2,3},{3,4},{4,5},{5,6},{6,7},{7,0},{8,9},{9,10},{10,1... | collective-permute-start | bytes 98312 | tf_op jit(solution)/shard_map/ppermute | solution.py:498
  123.1 5.6 %collective-permute-start.12 = (f32[24,2,128]{2,1,0:T(2,128)}, f32[24,2,128]{2,1,0:T(2,128)S(1)}, u32[]{:S(2)}, u32[]{:S(2)}) collective-permute-start(f32[24,2,128]{2,1,0:T(2,128)} %get-tuple-element.61), channel_id=1, source_target_pairs={{0,8},{8,16},{16,24},{24,32},{32,40},{40,48},{48,56},{56,64},{64,7... | collective-permute-start | bytes 73736 | tf_op jit(solution)/shard_map/ppermute | solution.py:498
  123.1 5.6 %collective-permute-start.13 = (f32[24,2,128]{2,1,0:T(2,128)}, f32[24,2,128]{2,1,0:T(2,128)S(1)}, u32[]{:S(2)}, u32[]{:S(2)}) collective-permute-start(f32[24,2,128]{2,1,0:T(2,128)} %get-tuple-element.62), channel_id=1, source_target_pairs={{0,120},{8,0},{16,8},{24,16},{32,24},{40,32},{48,40},{56,48},{64,5... | collective-permute-start | bytes 73736 | tf_op jit(solution)/shard_map/ppermute | solution.py:498
  128.6 2.2 %copy-start.23 = (f32[24,2,128]{2,1,0:T(2,128)}, f32[24,2,128]{2,1,0:T(2,128)S(1)}, u32[]{:S(2)}) copy-start(f32[24,2,128]{2,1,0:T(2,128)S(1)} %collective-permute-done.12.refs_13_) | copy-start | bytes 73732
  128.7 2.2 %copy-start.24 = (f32[24,2,128]{2,1,0:T(2,128)}, f32[24,2,128]{2,1,0:T(2,128)S(1)}, u32[]{:S(2)}) copy-start(f32[24,2,128]{2,1,0:T(2,128)S(1)} %collective-permute-done.13.refs_14_) | copy-start | bytes 73732
  128.7 2.2 %copy-start.20 = (f32[1,64,128]{2,1,0:T(8,128)}, f32[1,64,128]{2,1,0:T(8,128)S(1)}, u32[]{:S(2)}) copy-start(f32[1,64,128]{2,1,0:T(8,128)S(1)} %collective-permute-done.15.refs_16_) | copy-start | bytes 98308
  130.8 0.9 copy-start.2
  144.6 10.0 %collective-permute-start.19 = (f32[3,64,128]{2,1,0:T(8,128)}, f32[3,64,128]{2,1,0:T(8,128)S(1)}, u32[]{:S(2)}, u32[]{:S(2)}) collective-permute-start(f32[3,64,128]{2,1,0:T(8,128)} %get-tuple-element.70), channel_id=1, source_target_pairs={{0,7},{1,0},{2,1},{3,2},{4,3},{5,4},{6,5},{7,6},{8,15},{9,8},{10,9... | collective-permute-start | bytes 294920 | tf_op jit(solution)/shard_map/ppermute | solution.py:498
  148.2 8.4 %collective-permute-start.18 = (f32[3,64,128]{2,1,0:T(8,128)}, f32[3,64,128]{2,1,0:T(8,128)S(1)}, u32[]{:S(2)}, u32[]{:S(2)}) collective-permute-start(f32[3,64,128]{2,1,0:T(8,128)} %get-tuple-element.70), channel_id=1, source_target_pairs={{0,1},{1,2},{2,3},{3,4},{4,5},{5,6},{6,7},{7,0},{8,9},{9,10},{10,1... | collective-permute-start | bytes 294920 | tf_op jit(solution)/shard_map/ppermute | solution.py:498
  148.2 6.3 %collective-permute-start.16 = (f32[72,2,128]{2,1,0:T(2,128)}, f32[72,2,128]{2,1,0:T(2,128)S(1)}, u32[]{:S(2)}, u32[]{:S(2)}) collective-permute-start(f32[72,2,128]{2,1,0:T(2,128)} %get-tuple-element.68), channel_id=1, source_target_pairs={{0,8},{8,16},{16,24},{24,32},{32,40},{40,48},{48,56},{56,64},{64,7... | collective-permute-start | bytes 221192 | tf_op jit(solution)/shard_map/ppermute | solution.py:498
  148.2 6.3 %collective-permute-start.17 = (f32[72,2,128]{2,1,0:T(2,128)}, f32[72,2,128]{2,1,0:T(2,128)S(1)}, u32[]{:S(2)}, u32[]{:S(2)}) collective-permute-start(f32[72,2,128]{2,1,0:T(2,128)} %get-tuple-element.69), channel_id=1, source_target_pairs={{0,120},{8,0},{16,8},{24,16},{32,24},{40,32},{48,40},{56,48},{64,5... | collective-permute-start | bytes 221192 | tf_op jit(solution)/shard_map/ppermute | solution.py:498
  154.5 2.1 %copy-start.14 = (f32[72,2,128]{2,1,0:T(2,128)}, f32[72,2,128]{2,1,0:T(2,128)S(1)}, u32[]{:S(2)}) copy-start(f32[72,2,128]{2,1,0:T(2,128)S(1)} %collective-permute-done.16.refs_6_) | copy-start | bytes 221188
  154.5 2.1 %copy-start.15 = (f32[72,2,128]{2,1,0:T(2,128)}, f32[72,2,128]{2,1,0:T(2,128)S(1)}, u32[]{:S(2)}) copy-start(f32[72,2,128]{2,1,0:T(2,128)S(1)} %collective-permute-done.17.refs_7_) | copy-start | bytes 221188
  154.6 2.1 %copy-start.12 = (f32[3,64,128]{2,1,0:T(8,128)}, f32[3,64,128]{2,1,0:T(8,128)S(1)}, u32[]{:S(2)}) copy-start(f32[3,64,128]{2,1,0:T(8,128)S(1)} %collective-permute-done.19.refs_9_) | copy-start | bytes 294916
  156.7 0.6 copy-start.13
  (2 other events, 1.2 us)
